TPU v7x, 128 devices: a whole 4x4x4 slice. The times are simulated.
128 devices in a mesh: sec: 16 (over z_hi, x, core), tile: 8 (over z_lo, y).
Axes of the slice: x: 4, y: 4, z: 4 (z_hi: 2, z_lo: 2; z = z_hi * 2 + z_lo), core: 2. Of those that a mesh axis runs over, the one named last changes fastest.
Arguments:
- section_image: bfloat16 [32, 256, 1024], P('sec', 'tile'), may hold values from -6 to 6
- partner_row: int32 [32], P('sec'), may hold values from 0 to 31, as said below
- base_shift: int32 [32, 2, 128, 512], P('sec', None, 'tile'), may hold values from -4 to 3
- bilinear_frac: float32 [32, 2, 128, 512], P('sec', None, 'tile'), may hold values from 0 to 1
- first_kernel: bfloat16 [64, 16], replicated, may hold values from -1.5 to 1.5
- initial_conv_bias: float32 [64], replicated, may hold values from -3 to 3
- second_kernel: bfloat16 [64, 256], replicated, may hold values from -0.375 to 0.375
- second_bias: float32 [64], replicated, may hold values from -3 to 3
- edge_ends: int32 [32, 2, 2048], P('sec', None, 'tile'), may hold values from 0 to 255, as said below
- edge_count: int32 [32, 8], P('sec', 'tile'), may hold values from 64 to 256, as said below
- stiffness: float32 [32, 2048], P('sec', 'tile'), may hold values from 0.05 to 0.5
Outputs:
- correlation: bfloat16 [32, 81, 64, 256], P('sec', None, 'tile')
- mismatch: float32 [32, 128, 512], P('sec', 'tile')
- forces: float32 [32, 2, 256], P('sec', None, 'tile')
Inputs may be any that keep to these rules, and one draw needn't show every extreme that they name: Row p holds section z = (p mod 2) * 16 + floor(p / 2). partner_row[p] is the row of section z + 1, or of section z + 2 where section z + 1 is unusable, counted modulo 32. Among the 2 rows of every index of sec, both kinds occur. edge_ends[s, 1, e] is edge_ends[s, 0, e] plus 1, 32, 33 or 31, modulo 256. `edge_count`: in every section one block of slots is fully live and another has 64 live slots.
All inputs are finite; a program needn't handle non-finite values.
Results may differ from a plain program's by a relative error of at most 0.0036.
Values may be sent and summed in bfloat16 or wider, within the bound.
A program may use at most 128 MiB of HBM per device.

v0:
```python
import functools

import jax
import jax.numpy as jnp
import numpy as np
from jax import lax
from jax.experimental import pallas as pl
from jax.experimental.pallas import tpu as pltpu
from jax.sharding import PartitionSpec as P

BF = jnp.bfloat16
F32 = jnp.float32
MESH = pl.DeviceIdType.MESH
BIG = -1e30
VMEM_BYTES = 56 * 1024 * 1024

PT = 132
QUADS = PT // 4


def _tables():
    lane = np.arange(128)
    a, b, xx, yy = lane // 64, (lane // 32) % 2, (lane // 16) % 2, lane % 16
    x4, y2 = 2 * xx + b, 2 * yy + a
    ep = np.zeros((4, 96, 6, 128), np.float32)
    for p in range(6):
        ep[x4, 2 * y2 + 15 + p, p, lane] = 1
    oa, ob, ox, oy = lane // 64, (lane // 32) % 2, (lane // 8) % 4, lane % 8
    x8, y1 = 2 * ox + ob, 2 * oy + oa
    eo = np.zeros((8, 64, 6, 128), np.float32)
    for p in range(6):
        eo[x8, 2 * y1 + 15 + p, p, lane] = 1
    wsel = np.zeros((2, 2, 2, 16, 112), np.float32)
    wconst = np.zeros((2, 2, 2, 1, 112), np.float32)
    for e in range(2):
        for ta in range(2):
            for tb in range(2):
                for u in range(4):
                    for v in range(4):
                        wsel[e, ta, tb, 4 * u + v, (u + 2 * ta) * 16 + 8 * e + 2 * tb + v] = 1
                wconst[e, ta, tb, 0, 96 + 4 * e + 2 * ta + tb] = BIG
    extra = np.zeros((3, 3, 16, 256), np.float32)
    cmask = np.zeros((3, 3, 8, 128), np.float32)
    for tk in range(3):
        for gk, g in enumerate((0, 1, QUADS - 1)):
            for half in range(2):
                for e in range(2):
                    for ta in range(2):
                        for tb in range(2):
                            col = 4 * (4 * g + 2 * half + e) - 8 + x4 + tb
                            row = y2 - 8 + ta
                            bad = (col < 0) | (col > 511)
                            if tk == 0:
                                bad = bad | (row < 0)
                            if tk == 2:
                                bad = bad | (row > 15)
                            extra[tk, gk, 4 * e + 2 * ta + tb, 128 * half : 128 * half + 128] = bad
            extra[tk, gk, 8:11] = 1
            ccol, crow = 8 * g - 4 + lane // 16, lane % 16 - 4
            bad = (ccol < 0) | (ccol > 255)
            if tk == 0:
                bad = bad | (crow < 0)
            if tk == 2:
                bad = bad | (crow > 7)
            cmask[tk, gk] = np.where(bad, BIG, 0.0)
    src = np.arange(1024)
    unflat = np.zeros((1024, 1024), np.float32)
    unflat[src, (src % 8) * 128 + src // 8] = 1
    l2 = np.arange(256)
    lx = 8 * (l2 // 128) + 2 * ((l2 // 8) % 4) + (l2 // 32) % 2
    ly = 2 * (l2 % 8) + (l2 // 64) % 2
    home = np.stack([ly + 8, lx + 4]).astype(np.float32)
    return dict(
        ep=ep.reshape(384, 768),
        eo=eo.reshape(512, 768),
        wsel=wsel.reshape(8, 16, 112),
        wconst=wconst.reshape(8, 1, 112),
        extra=extra,
        cmask=cmask,
        unflat=unflat,
        home=home,
    )


def _split3(x):
    hi = x.astype(BF)
    rest = x - hi.astype(F32)
    mid = rest.astype(BF)
    low = (rest - mid.astype(F32)).astype(BF)
    return hi, mid, low


def _dot(x, y):
    return jnp.dot(x, y, preferred_element_type=F32)


def _comm_kernel(
    pr_ref, img_ref, anch_ref, ends_ref, cnt_ref, stiff_ref,
    j_ref, i_ref, f_ref,
    rbuf, gbuf, pbuf, pstage, send_sem, recv_sem,
):
    sec = lax.axis_index("sec")
    tile = lax.axis_index("tile")
    back1 = lax.rem(sec + 15, 16)
    back2 = lax.rem(sec + 14, 16)
    fwd1 = lax.rem(sec + 1, 16)
    fwd2 = lax.rem(sec + 2, 16)
    peers = [lax.rem(tile + r, 8) for r in range(8)]

    barrier = pltpu.get_barrier_semaphore()
    for other in (back1, back2, fwd1, fwd2):
        pl.semaphore_signal(barrier, inc=1, device_id=(other, tile), device_id_type=MESH)
    for r in range(1, 8):
        pl.semaphore_signal(barrier, inc=1, device_id=(sec, peers[r]), device_id_type=MESH)
    pl.semaphore_wait(barrier, 11)

    def remote(src, dst, k, target):
        return pltpu.make_async_remote_copy(
            src_ref=src, dst_ref=dst, send_sem=send_sem.at[k], recv_sem=recv_sem.at[k],
            device_id=target, device_id_type=MESH,
        )

    near = remote(img_ref, rbuf.at[0], 0, (back1, tile))
    far = remote(img_ref, rbuf.at[1], 1, (back2, tile))
    far.start()
    near.start()
    down_tile = (sec, lax.rem(tile + 1, 8))
    up_tile = (sec, lax.rem(tile + 7, 8))
    own_down = remote(img_ref.at[:, 16:32], i_ref.at[:, 0:16], 2, down_tile)
    own_up = remote(img_ref.at[:, 0:16], i_ref.at[:, 48:64], 3, up_tile)
    has_down = tile < 7
    has_up = tile > 0
    pl.when(has_down)(own_down.start)
    pl.when(has_up)(own_up.start)
    anchor_sends = [remote(anch_ref, gbuf.at[r], 4 + r, (sec, peers[r])) for r in range(1, 8)]
    for c in anchor_sends:
        c.start()

    i_ref[:, 16:48, :] = img_ref[...]

    @pl.when(tile == 0)
    def _():
        i_ref[:, 0:16, :] = jnp.zeros((2, 16, 1024), BF)
        j_ref[:, 0:32, :] = jnp.zeros((2, 32, 1024), BF)

    @pl.when(tile == 7)
    def _():
        i_ref[:, 48:64, :] = jnp.zeros((2, 16, 1024), BF)
        j_ref[:, 64:96, :] = jnp.zeros((2, 32, 1024), BF)

    near.wait()
    far.wait()
    for s in range(2):
        p = pr_ref[s]
        which = jnp.where(lax.shift_right_logical(p, 1) == fwd1, 0, 1)
        slot = lax.bitwise_and(p, 1)
        j_ref[s, 32:64, :] = rbuf[which, slot]
    part_down = remote(j_ref.at[:, 32:64], j_ref.at[:, 0:32], 12, down_tile)
    part_up = remote(j_ref.at[:, 32:64], j_ref.at[:, 64:96], 13, up_tile)
    pl.when(has_down)(part_down.start)
    pl.when(has_up)(part_up.start)

    for c in anchor_sends:
        c.wait()
    disp = anch_ref[...]
    for r in range(1, 8):
        disp = disp + gbuf[r]
    vert = lax.broadcasted_iota(jnp.int32, (256, 256), 0)
    live = lax.broadcasted_iota(jnp.int32, (2, 256), 1) < cnt_ref[...]
    stiff = jnp.where(live, stiff_ref[...], 0.0)
    row_of = lax.broadcasted_iota(jnp.int32, (8, 256), 0)
    parts = jnp.concatenate(_split3(disp), axis=0)
    total = jnp.zeros((8, 256), F32)
    for s in range(2):
        table = (vert == ends_ref[s, 1:2, :]).astype(F32) - (vert == ends_ref[s, 0:1, :]).astype(F32)
        table = table.astype(BF)
        got = _dot(parts, table)
        spread = (got[16:24] + got[8:16]) + got[0:8]
        pull = stiff[s : s + 1, :] * spread
        back = lax.dot_general(
            jnp.concatenate(_split3(pull), axis=0), table, (((1,), (1,)), ((), ())),
            preferred_element_type=F32,
        )
        back = (back[16:24] + back[8:16]) + back[0:8]
        total = total - jnp.where(lax.shift_right_logical(row_of, 1) == s, back, 0.0)
    pstage[...] = total
    force_sends = [remote(pstage, pbuf.at[r], 14 + r, (sec, peers[r])) for r in range(1, 8)]
    for c in force_sends:
        c.start()
    for c in force_sends:
        c.wait()
    for r in range(1, 8):
        total = total + pbuf[r]
    turned = pltpu.roll(total, lax.rem(256 - 32 * tile, 256), 1)
    f_ref[...] = turned[:, 0:128]

    pl.when(has_down)(own_down.wait_send)
    pl.when(has_up)(own_up.wait_send)
    pl.when(has_up)(own_down.wait_recv)
    pl.when(has_down)(own_up.wait_recv)
    pl.when(has_down)(part_down.wait_send)
    pl.when(has_up)(part_up.wait_send)
    pl.when(has_up)(part_down.wait_recv)
    pl.when(has_down)(part_up.wait_recv)


def _exchange(partner_row, image, anchors, ends, count, stiffness):
    vm = pl.BlockSpec(memory_space=pltpu.VMEM)
    return pl.pallas_call(
        _comm_kernel,
        out_shape=(
            jax.ShapeDtypeStruct((2, 96, 1024), BF),
            jax.ShapeDtypeStruct((2, 64, 1024), BF),
            jax.ShapeDtypeStruct((8, 128), F32),
        ),
        in_specs=[pl.BlockSpec(memory_space=pltpu.SMEM)] + [vm] * 5,
        out_specs=(vm, vm, vm),
        scratch_shapes=[
            pltpu.VMEM((2, 2, 32, 1024), BF),
            pltpu.VMEM((8, 8, 256), F32),
            pltpu.VMEM((8, 8, 256), F32),
            pltpu.VMEM((8, 256), F32),
            pltpu.SemaphoreType.DMA((22,)),
            pltpu.SemaphoreType.DMA((22,)),
        ],
        compiler_params=pltpu.CompilerParams(
            collective_id=0, has_side_effects=True, vmem_limit_bytes=24 * 1024 * 1024
        ),
        name="exchange",
    )(partner_row, image, anchors, ends, count, stiffness)


def _work_kernel(
    tk_ref, j_ref, i_ref, sh_ref, fr_ref, w1_ref, b1_ref, w2_ref, b2_ref,
    ep_ref, eo_ref, wsel_ref, wconst_ref, extra_ref, cmask_ref, unflat_ref, home_ref,
    corr_ref, mis_ref,
    pad, qp, qo, p4, cpt, obuf, cbuf, wq,
):
    tk = tk_ref[0]
    lane = lax.broadcasted_iota(jnp.int32, (64, 112), 1)
    hi, mid, low = (x.astype(F32) for x in _split3(b1_ref[...]))
    base = (
        jnp.where(lane == 104, hi, 0.0) + jnp.where(lane == 105, mid, 0.0) + jnp.where(lane == 106, low, 0.0)
    )
    for m in range(8):
        wq[64 * m : 64 * m + 64, :] = (_dot(w1_ref[...], wsel_ref[m]) + base + wconst_ref[m]).astype(BF)

    lane128 = lax.broadcasted_iota(jnp.int32, (1, 128), 1)
    x_bit = [lax.bitwise_and(lax.shift_right_logical(lane128, 3 + k), 1) == 1 for k in range(4)]
    y_bit = [lax.bitwise_and(lax.shift_right_logical(lane128, k), 1) == 1 for k in range(3)]
    row16 = lax.broadcasted_iota(jnp.int32, (16, 256), 0)

    def section(s, carry):
        pad[0:64, 0:1024] = i_ref[s].astype(F32)
        pad[0:96, 1024:1152] = jnp.zeros((96, 128), F32)
        wide = pad[0:64, :]
        stack = jnp.concatenate(
            [pltpu.roll(wide, (1 - 2 * k) % 1152, 1)[:, 0:1024] for k in range(8)], axis=0
        )
        qo[...] = _dot(stack.T.astype(BF), eo_ref[...]).astype(BF)
        pad[0:96, 0:1024] = j_ref[s].astype(F32)
        wide = pad[...]
        stack = jnp.concatenate([pltpu.roll(wide, (17 - 2 * k) % 1152, 1) for k in range(4)], axis=0)
        qp[...] = _dot(stack.T.astype(BF), ep_ref[...])[0:1056].astype(BF)

        def partner(g, carry):
            r0 = pl.multiple_of(32 * g, 32)
            left = qp[pl.ds(r0, 16), :]
            right = qp[pl.ds(r0 + 16, 16), :]
            kind = jnp.where(g == 0, 0, jnp.where(g == QUADS - 1, 2, 1))
            patches = jnp.concatenate(
                [
                    jnp.concatenate([left[:, 128 * p : 128 * p + 128], right[:, 128 * p : 128 * p + 128]], axis=1)
                    for p in range(6)
                ]
                + [extra_ref[tk, kind]],
                axis=0,
            )
            got = jnp.maximum(_dot(wq[...], patches).astype(BF), 0)
            l0 = pl.multiple_of(512 * g, 512)
            quad = jnp.concatenate(
                [got[0:256, 0:128], got[256:512, 0:128], got[0:256, 128:256], got[256:512, 128:256]], axis=1
            )
            p4[:, pl.ds(l0, 512)] = quad
            pre = _dot(w2_ref[...], quad)
            pre = jnp.concatenate([pre[:, 128 * k : 128 * k + 32] for k in range(4)], axis=1)
            coarse = jnp.maximum(pre + b2_ref[...] + cmask_ref[tk, kind][0:1, :], 0.0)
            coarse = coarse.astype(BF).astype(F32)
            cpt[pl.ds(pl.multiple_of(128 * g, 128), 128), 0:64] = coarse.T.astype(BF)
            return carry

        lax.fori_loop(0, QUADS, partner, 0)

        def block(c, carry):
            coarse_parts = []
            for half in range(2):
                b = 2 * c + half
                r0 = pl.multiple_of(32 * b, 32)
                left = qo[pl.ds(r0, 16), :]
                right = qo[pl.ds(r0 + 16, 16), :]
                patches = jnp.concatenate(
                    [
                        jnp.concatenate([left[:, 128 * p : 128 * p + 128], right[:, 128 * p : 128 * p + 128]], axis=1)
                        for p in range(6)
                    ]
                    + [extra_ref[1, 1]],
                    axis=0,
                )
                own4 = jnp.maximum(_dot(wq[0:256, :], patches).astype(BF), 0)
                own = own4[0:64, :].astype(F32)
                pre = _dot(w2_ref[...], own4)
                coarse_parts += [pre[:, 0:32], pre[:, 128:160]]

                row = home_ref[0:1, :] + sh_ref[s, 0, pl.ds(b, 1), :].astype(F32)
                col = home_ref[1:2, :] + sh_ref[s, 1, pl.ds(b, 1), :].astype(F32)
                fy = fr_ref[s, 0, pl.ds(b, 1), :]
                fx = fr_ref[s, 1, pl.ds(b, 1), :]
                row = jnp.broadcast_to(row.astype(jnp.int32), (16, 256))
                col = jnp.broadcast_to(col, (16, 256)).astype(BF)
                oy = [(row == 2 * row16 + a).astype(F32).astype(BF) for a in range(2)]
                zero = jnp.zeros((16, 256), BF)
                picks = []
                for k in range(6):
                    hit = {}
                    for bb in range(2):
                        for xx in range(2):
                            hit[bb, xx] = col == float(4 * k + 2 * xx + bb)
                    for a in range(2):
                        for bb in range(2):
                            for xx in range(2):
                                picks.append(jnp.where(hit[bb, xx], oy[a], zero))
                choose = jnp.concatenate(picks, axis=0)
                l0 = pl.multiple_of(512 * b + 128, 128)
                taps = _dot(p4[:, pl.ds(l0, 768)], choose)
                gy, gx = 1.0 - fy, 1.0 - fx
                warped = (
                    (gy * gx) * taps[0:64] + (gy * fx) * taps[64:128]
                    + (fy * gx) * taps[128:192] + (fy * fx) * taps[192:256]
                )
                differ = own - warped
                mis_ref[s, pl.ds(b, 1), :] = jnp.sum(differ * differ, axis=0, keepdims=True) * (1.0 / 64)

            coarse = jnp.maximum(jnp.concatenate(coarse_parts, axis=1) + b2_ref[...], 0.0).astype(BF)
            near = cpt[pl.ds(pl.multiple_of(256 * c, 256), 384), 0:64]
            gram = _dot(near, coarse).reshape(24, 16, 128)
            for k, keep in ((3, 16), (2, 12), (1, 10), (0, 9)):
                step = 1 << k
                gram = jnp.where(x_bit[k][None], gram[step : step + keep], gram[0:keep])
            gram = gram.reshape(144, 128)
            cols = []
            for j in range(9):
                v = gram[16 * j : 16 * j + 16]
                for k in (2, 1, 0):
                    v = jnp.where(y_bit[k], pltpu.roll(v, 16 - (1 << k), 0), v)
                cols.append(v)
            gram = jnp.concatenate(cols, axis=0) * (1.0 / 64)
            obuf[:, pl.ds(pl.multiple_of(128 * c, 128), 128)] = gram.astype(BF)
            return carry

        lax.fori_loop(0, 16, block, 0)

        for h in range(2):
            flat = _dot(obuf[:, 1024 * h : 1024 * h + 1024], unflat_ref[...])
            for j in range(9):
                for y in range(8):
                    cbuf[h, pl.ds(8 * j + y, 9, stride=72), :] = flat[16 * j : 16 * j + 9, 128 * y : 128 * y + 128]
        for h in range(2):
            corr_ref[s, :, :, 128 * h : 128 * h + 128] = cbuf[h].reshape(81, 8, 128).astype(BF)
        return carry

    lax.fori_loop(0, 2, section, 0)


def _work(tile_kind, j, i, shift_px, frac_px, w1, b1, w2, b2, interpret=False):
    t = _tables()
    vm = pl.BlockSpec(memory_space=pltpu.VMEM)
    consts = [
        jnp.asarray(t["ep"], BF), jnp.asarray(t["eo"], BF), jnp.asarray(t["wsel"], BF),
        jnp.asarray(t["wconst"], F32), jnp.asarray(t["extra"], BF), jnp.asarray(t["cmask"], F32),
        jnp.asarray(t["unflat"], BF), jnp.asarray(t["home"], F32),
    ]
    return pl.pallas_call(
        _work_kernel,
        out_shape=(
            jax.ShapeDtypeStruct((2, 81, 8, 256), BF),
            jax.ShapeDtypeStruct((2, 32, 256), F32),
        ),
        in_specs=[pl.BlockSpec(memory_space=pltpu.SMEM)] + [vm] * 16,
        out_specs=(vm, vm),
        scratch_shapes=[
            pltpu.VMEM((96, 1152), F32),
            pltpu.VMEM((1056, 768), BF),
            pltpu.VMEM((1024, 768), BF),
            pltpu.VMEM((256, PT * 128), BF),
            pltpu.VMEM((PT * 32, 128), BF),
            pltpu.VMEM((144, 2048), BF),
            pltpu.VMEM((2, 648, 128), F32),
            pltpu.VMEM((512, 112), BF),
        ],
        compiler_params=pltpu.CompilerParams(vmem_limit_bytes=VMEM_BYTES),
        interpret=interpret,
        name="work",
    )(tile_kind, j, i, shift_px, frac_px, w1, b1, w2, b2, *consts)


def _to_px(x):
    x = x.reshape(2, 2, 8, 2, 32, 2, 4, 2)
    return x.transpose(0, 1, 4, 5, 3, 7, 6, 2).reshape(2, 2, 32, 256)


def _from_px(x):
    x = x.reshape(2, 32, 2, 2, 2, 4, 8)
    return x.transpose(0, 6, 3, 1, 2, 5, 4).reshape(2, 16, 512)


def local(
    section_image, partner_row, base_shift, bilinear_frac, first_kernel, initial_conv_bias,
    second_kernel, second_bias, edge_ends, edge_count, stiffness,
):
    tile = lax.axis_index("tile")
    anchors = base_shift[:, :, 0, ::16].astype(F32) + bilinear_frac[:, :, 0, ::16]
    anchors = jnp.pad(anchors.reshape(4, 32), ((0, 4), (0, 224)))
    lanes = lax.broadcasted_iota(jnp.int32, (8, 256), 1)
    anchors = jnp.where(lanes // 32 == tile, jnp.tile(anchors[:, 0:32], (1, 8)), 0.0)
    j, i, force = _exchange(partner_row, section_image, anchors, edge_ends, edge_count, stiffness)
    kind = jnp.where(tile == 0, 0, jnp.where(tile == 7, 2, 1)).astype(jnp.int32).reshape(1)
    corr, mis = _work(
        kind, j, i, _to_px(base_shift), _to_px(bilinear_frac), first_kernel,
        initial_conv_bias.reshape(64, 1), second_kernel, second_bias.reshape(64, 1),
    )
    return corr, _from_px(mis), force[0:4, 0:32].reshape(2, 2, 32)


def solution(mesh):
    in_specs = (
        P("sec", "tile", None), P("sec"), P("sec", None, "tile", None), P("sec", None, "tile", None),
        P(), P(), P(), P(), P("sec", None, "tile"), P("sec", "tile"), P("sec", "tile"),
    )
    out_specs = (P("sec", None, "tile", None), P("sec", "tile", None), P("sec", None, "tile"))
    return jax.shard_map(local, mesh=mesh, in_specs=in_specs, out_specs=out_specs, check_vma=False)
```

profile of v0, /device:TPU:15, one launch (start us, length us, event | category | flops | bytes accessed | tf_op | source)
XLA Modules:
  0.0 154.0 jit_solution(16498259710987921464)
XLA Ops:
  0.6 1.0 slice.12
  1.6 1.0 slice.13
  2.7 0.1 tile.10
  2.8 0.7 copy.29.cnt_ref
  3.5 0.0 copy-start.2
  3.5 0.9 copy-done.2
  4.4 0.7 copy-done.3
  5.1 0.0 copy-start.4
  5.1 0.7 copy-done.4
  5.8 0.7 copy-done.5
  6.5 20.2 %exchange.1 = (bf16[2,96,1024]{2,1,0:T(8,128)(2,1)S(1)}, bf16[2,64,1024]{2,1,0:T(8,128)(2,1)S(1)}, f32[8,128]{1,0:T(8,128)S(1)}) custom-call(s32[2]{0:T(128)S(1)} %copy-done.5, bf16[2,32,1024]{2,1,0:T(8,128)(2,1)S(1)} %copy-done.2, f32[8,256]{1,0:T(8,128)S(1)} %fusion.anch_ref, s32[2,2,256]{2,1,0:T(2,128)S(1)} %copy-done.3, s32[2,1]{1,0:T(2,128)S(1)} %copy.29.cnt_ref, ...), custom_call_target="tpu_custom_call" | custom-call | tf_op jit(solution)/shard_map/exchange/pallas_call | solution.py:209
  26.7 0.0 copy-start
  26.7 0.8 copy-done
  27.5 0.7 copy-done.1
  28.2 12.8 %reshape.46 = s32[2,2,8,2,32,2,4,2]{7,6,5,4,3,2,1,0:T(4,128)} reshape(s32[2,2,16,512]{3,2,1,0:T(8,128)} %param.21) | data formatting | bytes 262144 | tf_op jit(solution)/shard_map/reshape | solution.py:407
  41.1 7.5 %copy.30 = s32[2,2,32,2,2,2,4,8]{2,7,6,5,4,3,1,0:T(8,128)S(1)} copy(s32[2,2,32,2,2,2,4,8]{5,6,3,2,4,7,1,0:T(4,128)} %bitcast.16) | data formatting | bytes 262144 | tf_op jit(solution)/shard_map/transpose | solution.py:408
  48.6 0.8 copy.32.sh_ref
  49.4 0.0 copy-done.6
  49.4 12.0 %reshape.48 = f32[2,2,8,2,32,2,4,2]{7,6,5,4,3,2,1,0:T(4,128)} reshape(f32[2,2,16,512]{3,2,1,0:T(8,128)S(1)} %copy-done.6) | data formatting | bytes 262144 | tf_op jit(solution)/shard_map/reshape | solution.py:407
  61.5 7.5 %copy.31 = f32[2,2,32,2,2,2,4,8]{2,7,6,5,4,3,1,0:T(8,128)S(1)} copy(f32[2,2,32,2,2,2,4,8]{5,6,3,2,4,7,1,0:T(4,128)} %bitcast.17) | data formatting | bytes 262144 | tf_op jit(solution)/shard_map/transpose | solution.py:408
  69.0 0.8 copy.33.fr_ref
  69.8 0.0 copy-done.8
  69.8 0.7 copy.35.b1_ref
  70.6 0.0 copy-done.9
  70.6 0.7 copy.36.b2_ref
  71.3 0.0 copy-done.7
  71.3 0.7 copy.34.w1_ref
  71.9 70.9 %work.1 = (bf16[2,81,8,256]{3,2,1,0:T(8,128)(2,1)}, f32[2,32,256]{2,1,0:T(8,128)}) custom-call(s32[1]{0:T(128)} %bitcast.tk_ref, bf16[2,96,1024]{2,1,0:T(8,128)(2,1)} %copy-done, bf16[2,64,1024]{2,1,0:T(8,128)(2,1)} %copy-done.1, s32[2,2,32,256]{3,2,1,0:T(8,128)} %copy.32.sh_ref, f32[2,2,32,256]{3,2,1,0:T(8,128)} %copy.33.fr_ref, ...), custom_call_target="tpu_custom_call" | custom-call | tf_op jit(solution)/shard_map/work/pallas_call | solution.py:382
  142.8 1.0 copy.37
  143.8 3.4 %copy.38 = f32[2,8,2,32,2,4,2]{6,5,4,3,2,1,0:T(4,128)} copy(f32[2,8,2,32,2,4,2]{3,1,5,6,2,4,0:T(8,128)S(1)} %bitcast.20) | data formatting | bytes 131072 | tf_op jit(solution)/shard_map/transpose | solution.py:413
  147.2 6.3 %reshape.53 = f32[2,16,512]{2,1,0:T(8,128)} reshape(f32[2,8,2,32,2,4,2]{6,5,4,3,2,1,0:T(4,128)} %copy.38) | data formatting | bytes 131072 | tf_op jit(solution)/shard_map/reshape | solution.py:413
  153.4 0.6 slice.15
  (13 shorter events, 0.0 us)
Async XLA Ops:
  3.5 0.9 copy-start.2
  4.4 0.7 copy-start.3
  5.1 0.7 copy-start.4
  5.8 0.7 copy-start.5
  26.7 0.8 copy-start
  27.5 0.7 copy-start.1
  28.2 21.2 %copy-start.6 = (f32[2,2,16,512]{3,2,1,0:T(8,128)S(1)}, f32[2,2,16,512]{3,2,1,0:T(8,128)}, u32[]{:S(2)}) copy-start(f32[2,2,16,512]{3,2,1,0:T(8,128)} %param.22) | copy-start | bytes 393220
  49.4 20.4 %copy-start.8 = (f32[64]{0:T(128)S(1)}, f32[64]{0:T(128)}, u32[]{:S(2)}) copy-start(f32[64]{0:T(128)} %param.24) | copy-start | bytes 772
  49.4 21.1 %copy-start.9 = (f32[64]{0:T(128)S(1)}, f32[64]{0:T(128)}, u32[]{:S(2)}) copy-start(f32[64]{0:T(128)} %param.26) | copy-start | bytes 772
  49.4 21.8 %copy-start.7 = (bf16[64,16]{0,1:T(8,128)(2,1)S(1)}, bf16[64,16]{0,1:T(8,128)(2,1)}, u32[]{:S(2)}) copy-start(bf16[64,16]{0,1:T(8,128)(2,1)} %param.23) | copy-start | bytes 6148
where the time goes:
time: 155 us; the launch traced here: 154 us
  Pallas kernels  91.1 us (59%)
  local copies, waits for them, and re-layouts  62.1 us (40%)
    pallas_call x1, Pallas kernels, _work(): pl.pallas_call(_work_kernel, out_shape=(jax.ShapeDtypeStruct((2, 81, 8, 2...  70.9 us
    reshape x2, local copies, waits for them, and re-layouts, _to_px(): x = x.reshape(2, 2, 8, 2, 32, 2, 4, 2)  24.9 us
    pallas_call x1, Pallas kernels, _exchange(): pl.pallas_call(_comm_kernel, out_shape=(jax.ShapeDtypeStruct((2, 96, 1024...  20.2 us
    transpose x2, local copies, waits for them, and re-layouts, _to_px(): return x.transpose(0, 1, 4, 5, 3, 7, 6, 2).reshape(2, 2, 32, 256)  15.1 us
    reshape x1, local copies, waits for them, and re-layouts, _from_px(): return x.transpose(0, 6, 3, 1, 2, 5, 4).reshape(2, 16, 512)  6.26 us
    unnamed x22, local copies, waits for them, and re-layouts  5.86 us
    transpose x1, local copies, waits for them, and re-layouts, _from_px(): return x.transpose(0, 6, 3, 1, 2, 5, 4).reshape(2, 16, 512)  3.41 us

commit v1 on v0

--- a/solution.py
+++ b/solution.py
@@ -69,6 +69,8 @@
     l2 = np.arange(256)
     lx = 8 * (l2 // 128) + 2 * ((l2 // 8) % 4) + (l2 // 32) % 2
     ly = 2 * (l2 % 8) + (l2 // 64) % 2
+    perm = np.zeros((256, 256), np.float32)
+    perm[16 * lx + ly, l2] = 1
     home = np.stack([ly + 8, lx + 4]).astype(np.float32)
     return dict(
         ep=ep.reshape(384, 768),
@@ -79,6 +81,7 @@
         cmask=cmask,
         unflat=unflat,
         home=home,
+        perm=perm,
     )
 
 
@@ -232,9 +235,9 @@
 
 def _work_kernel(
     tk_ref, j_ref, i_ref, sh_ref, fr_ref, w1_ref, b1_ref, w2_ref, b2_ref,
-    ep_ref, eo_ref, wsel_ref, wconst_ref, extra_ref, cmask_ref, unflat_ref, home_ref,
+    ep_ref, eo_ref, wsel_ref, wconst_ref, extra_ref, cmask_ref, unflat_ref, home_ref, perm_ref,
     corr_ref, mis_ref,
-    pad, qp, qo, p4, cpt, obuf, cbuf, wq,
+    pad, qp, qo, p4, cpt, obuf, cbuf, wq, tbuf, px, mpx,
 ):
     tk = tk_ref[0]
     lane = lax.broadcasted_iota(jnp.int32, (64, 112), 1)
@@ -251,6 +254,17 @@
     row16 = lax.broadcasted_iota(jnp.int32, (16, 256), 0)
 
     def section(s, carry):
+        planes = [sh_ref[s, k].astype(F32) for k in range(2)] + [fr_ref[s, k] for k in range(2)]
+        tbuf[:, 0:64] = jnp.concatenate(planes, axis=0).T
+        runs = [tbuf[pl.ds(x, 32, stride=16), :] for x in range(16)]
+        planes = [jnp.concatenate([r[:, 16 * k : 16 * k + 16] for r in runs], axis=1) for k in range(4)]
+        parts = [planes[0].astype(BF), planes[1].astype(BF), *_split3(planes[2]), *_split3(planes[3])]
+        got = _dot(jnp.concatenate(parts, axis=0), perm_ref[...])
+        px[0] = got[0:32] + home_ref[0:1, :]
+        px[1] = got[32:64] + home_ref[1:2, :]
+        px[2] = (got[128:160] + got[96:128]) + got[64:96]
+        px[3] = (got[224:256] + got[192:224]) + got[160:192]
+
         pad[0:64, 0:1024] = i_ref[s].astype(F32)
         pad[0:96, 1024:1152] = jnp.zeros((96, 128), F32)
         wide = pad[0:64, :]
@@ -282,14 +296,26 @@
                 [got[0:256, 0:128], got[256:512, 0:128], got[0:256, 128:256], got[256:512, 128:256]], axis=1
             )
             p4[:, pl.ds(l0, 512)] = quad
-            pre = _dot(w2_ref[...], quad)
-            pre = jnp.concatenate([pre[:, 128 * k : 128 * k + 32] for k in range(4)], axis=1)
-            coarse = jnp.maximum(pre + b2_ref[...] + cmask_ref[tk, kind][0:1, :], 0.0)
-            coarse = coarse.astype(BF).astype(F32)
-            cpt[pl.ds(pl.multiple_of(128 * g, 128), 128), 0:64] = coarse.T.astype(BF)
             return carry
 
-        lax.fori_loop(0, QUADS, partner, 0)
+        lax.fori_loop(0, QUADS, partner, 0, unroll=3)
+
+        def coarsen(q, count):
+            tiles = p4[:, pl.ds(pl.multiple_of(512 * q, 512), 512 * count)]
+            tiles = jnp.concatenate([tiles[:, 128 * k : 128 * k + 32] for k in range(4 * count)], axis=1)
+            pre = _dot(w2_ref[...], tiles) + b2_ref[...]
+            for n in range(count):
+                kind = jnp.where(q + n == 0, 0, jnp.where(q + n == QUADS - 1, 2, 1))
+                coarse = jnp.maximum(pre[:, 128 * n : 128 * n + 128] + cmask_ref[tk, kind][0:1, :], 0.0)
+                coarse = coarse.astype(BF).astype(F32)
+                cpt[pl.ds(pl.multiple_of(128 * (q + n), 128), 128), 0:64] = coarse.T.astype(BF)
+
+        def coarsen_pair(g, carry):
+            coarsen(2 * g, 2)
+            return carry
+
+        lax.fori_loop(0, QUADS // 2, coarsen_pair, 0, unroll=2)
+        coarsen(QUADS - 1, 1)
 
         def block(c, carry):
             coarse_parts = []
@@ -311,10 +337,10 @@
                 pre = _dot(w2_ref[...], own4)
                 coarse_parts += [pre[:, 0:32], pre[:, 128:160]]
 
-                row = home_ref[0:1, :] + sh_ref[s, 0, pl.ds(b, 1), :].astype(F32)
-                col = home_ref[1:2, :] + sh_ref[s, 1, pl.ds(b, 1), :].astype(F32)
-                fy = fr_ref[s, 0, pl.ds(b, 1), :]
-                fx = fr_ref[s, 1, pl.ds(b, 1), :]
+                row = px[0, pl.ds(b, 1), :]
+                col = px[1, pl.ds(b, 1), :]
+                fy = px[2, pl.ds(b, 1), :]
+                fx = px[3, pl.ds(b, 1), :]
                 row = jnp.broadcast_to(row.astype(jnp.int32), (16, 256))
                 col = jnp.broadcast_to(col, (16, 256)).astype(BF)
                 oy = [(row == 2 * row16 + a).astype(F32).astype(BF) for a in range(2)]
@@ -338,7 +364,7 @@
                     + (fy * gx) * taps[128:192] + (fy * fx) * taps[192:256]
                 )
                 differ = own - warped
-                mis_ref[s, pl.ds(b, 1), :] = jnp.sum(differ * differ, axis=0, keepdims=True) * (1.0 / 64)
+                mpx[pl.ds(b, 1), :] = jnp.sum(differ * differ, axis=0, keepdims=True) * (1.0 / 64)
 
             coarse = jnp.maximum(jnp.concatenate(coarse_parts, axis=1) + b2_ref[...], 0.0).astype(BF)
             near = cpt[pl.ds(pl.multiple_of(256 * c, 256), 384), 0:64]
@@ -359,6 +385,15 @@
 
         lax.fori_loop(0, 16, block, 0)
 
+        got = lax.dot_general(
+            jnp.concatenate(_split3(mpx[...]), axis=0), perm_ref[...], (((1,), (1,)), ((), ())),
+            preferred_element_type=F32,
+        )
+        got = (got[64:96] + got[32:64]) + got[0:32]
+        for x in range(16):
+            tbuf[pl.ds(x, 32, stride=16), 0:16] = got[:, 16 * x : 16 * x + 16]
+        mis_ref[s] = tbuf[...].T[0:16, :]
+
         for h in range(2):
             flat = _dot(obuf[:, 1024 * h : 1024 * h + 1024], unflat_ref[...])
             for j in range(9):
@@ -371,21 +406,22 @@
     lax.fori_loop(0, 2, section, 0)
 
 
-def _work(tile_kind, j, i, shift_px, frac_px, w1, b1, w2, b2, interpret=False):
+def _work(tile_kind, j, i, shift, frac, w1, b1, w2, b2, interpret=False):
     t = _tables()
     vm = pl.BlockSpec(memory_space=pltpu.VMEM)
     consts = [
         jnp.asarray(t["ep"], BF), jnp.asarray(t["eo"], BF), jnp.asarray(t["wsel"], BF),
         jnp.asarray(t["wconst"], F32), jnp.asarray(t["extra"], BF), jnp.asarray(t["cmask"], F32),
         jnp.asarray(t["unflat"], BF), jnp.asarray(t["home"], F32),
+        jnp.asarray(t["perm"], BF),
     ]
     return pl.pallas_call(
         _work_kernel,
         out_shape=(
             jax.ShapeDtypeStruct((2, 81, 8, 256), BF),
-            jax.ShapeDtypeStruct((2, 32, 256), F32),
+            jax.ShapeDtypeStruct((2, 16, 512), F32),
         ),
-        in_specs=[pl.BlockSpec(memory_space=pltpu.SMEM)] + [vm] * 16,
+        in_specs=[pl.BlockSpec(memory_space=pltpu.SMEM)] + [vm] * 17,
         out_specs=(vm, vm),
         scratch_shapes=[
             pltpu.VMEM((96, 1152), F32),
@@ -396,21 +432,14 @@
             pltpu.VMEM((144, 2048), BF),
             pltpu.VMEM((2, 648, 128), F32),
             pltpu.VMEM((512, 112), BF),
+            pltpu.VMEM((512, 128), F32),
+            pltpu.VMEM((4, 32, 256), F32),
+            pltpu.VMEM((32, 256), F32),
         ],
         compiler_params=pltpu.CompilerParams(vmem_limit_bytes=VMEM_BYTES),
         interpret=interpret,
         name="work",
-    )(tile_kind, j, i, shift_px, frac_px, w1, b1, w2, b2, *consts)
-
-
-def _to_px(x):
-    x = x.reshape(2, 2, 8, 2, 32, 2, 4, 2)
-    return x.transpose(0, 1, 4, 5, 3, 7, 6, 2).reshape(2, 2, 32, 256)
-
-
-def _from_px(x):
-    x = x.reshape(2, 32, 2, 2, 2, 4, 8)
-    return x.transpose(0, 6, 3, 1, 2, 5, 4).reshape(2, 16, 512)
+    )(tile_kind, j, i, shift, frac, w1, b1, w2, b2, *consts)
 
 
 def local(
@@ -425,10 +454,10 @@
     j, i, force = _exchange(partner_row, section_image, anchors, edge_ends, edge_count, stiffness)
     kind = jnp.where(tile == 0, 0, jnp.where(tile == 7, 2, 1)).astype(jnp.int32).reshape(1)
     corr, mis = _work(
-        kind, j, i, _to_px(base_shift), _to_px(bilinear_frac), first_kernel,
+        kind, j, i, base_shift, bilinear_frac, first_kernel,
         initial_conv_bias.reshape(64, 1), second_kernel, second_bias.reshape(64, 1),
     )
-    return corr, _from_px(mis), force[0:4, 0:32].reshape(2, 2, 32)
+    return corr, mis, force[0:4, 0:32].reshape(2, 2, 32)
 
 
 def solution(mesh):

time: 155 us -> 82.9 us (0.53)
  local copies, waits for them, and re-layouts: 62.1 us -> 11.8 us
  Pallas kernels: 91.1 us -> 70 us
    reshape x5 -> x0, local copies, waits for them, and re-layouts: 32.8 us -> none  [the longest x2 24.9 us: _to_px(): x = x.reshape(2, 2, 8, 2, 32, 2, 4, 2)]
    pallas_call x1, Pallas kernels: 70.9 us -> 49.7 us  [_work(): pl.pallas_call(_work_kernel, out_shape=(jax.ShapeDtypeStruct((2, 81, 8, 2...]
    transpose x3 -> x0, local copies, waits for them, and re-layouts: 18.5 us -> none  [the longest x2 15.1 us: _to_px(): return x.transpose(0, 1, 4, 5, 3, 7, 6, 2).reshape(2, 2, 32, 256)]
    unnamed x22 -> x14, local copies, waits for them, and re-layouts: 5.86 us -> 6.46 us
where the time goes in v1:
time: 82.9 us; the launch traced here: 82.5 us
  Pallas kernels  70 us (84%)
  local copies, waits for them, and re-layouts  11.8 us (14%)
    pallas_call x1, Pallas kernels, _work(): pl.pallas_call(_work_kernel, out_shape=(jax.ShapeDtypeStruct((2, 81, 8, 2...  49.7 us
    pallas_call x1, Pallas kernels, _exchange(): pl.pallas_call(_comm_kernel, out_shape=(jax.ShapeDtypeStruct((2, 96, 1024...  20.2 us
    unnamed x14, local copies, waits for them, and re-layouts  6.46 us

profile of v1, /device:TPU:15, one launch (start us, length us, event | category | flops | bytes accessed | tf_op | source)
XLA Modules:
  0.0 82.5 jit_solution(9254173650557201941)
XLA Ops:
  0.7 0.7 copy.23.cnt_ref
  1.4 1.0 %slice.12 = s32[2,2,1,32]{3,2,1,0:T(1,128)S(1)} slice(s32[2,2,16,512]{3,2,1,0:T(8,128)} %sh_ref.1), slice={[0:2:1], [0:2:1], [0:1:1], [0:512:16]} | slice | bytes 1024 | tf_op jit(solution)/shard_map/slice | solution.py:450
  2.4 1.0 %slice.13 = f32[2,2,1,32]{3,2,1,0:T(1,128)S(1)} slice(f32[2,2,16,512]{3,2,1,0:T(8,128)} %fr_ref.1), slice={[0:2:1], [0:2:1], [0:1:1], [0:512:16]} | slice | bytes 1024 | tf_op jit(solution)/shard_map/slice | solution.py:450
  3.4 1.4 %copy.24.w1_ref = bf16[64,16]{1,0:T(8,128)(2,1)} copy(bf16[64,16]{0,1:T(8,128)(2,1)} %param.24) | data formatting | bytes 4096 | tf_op args[4]
  4.8 0.1 tile.10
  4.9 1.4 %copy.25.b1_ref = f32[64,1]{1,0:T(8,128)} copy(f32[64,1]{0,1:T(1,128)} %bitcast.7) | data formatting | bytes 512 | tf_op jit(solution)/shard_map/reshape | solution.py:458
  6.3 1.4 %copy.26.b2_ref = f32[64,1]{1,0:T(8,128)} copy(f32[64,1]{0,1:T(1,128)} %bitcast.8) | data formatting | bytes 512 | tf_op jit(solution)/shard_map/reshape | solution.py:458
  7.6 0.0 copy-start.2
  7.6 0.9 %copy-done.2 = bf16[2,32,1024]{2,1,0:T(8,128)(2,1)S(1)} copy-done((bf16[2,32,1024]{2,1,0:T(8,128)(2,1)S(1)}, bf16[2,32,1024]{2,1,0:T(8,128)(2,1)}, u32[]{:S(2)}) %copy-start.2) | copy-done | bytes 131096
  8.5 0.0 copy-start.3
  8.5 0.7 copy-done.3
  9.2 0.0 copy-start.4
  9.2 0.7 copy-done.4
  9.9 0.0 copy-start.5
  9.9 0.7 copy-done.5
  10.5 20.2 %exchange.1 = (bf16[2,96,1024]{2,1,0:T(8,128)(2,1)S(1)}, bf16[2,64,1024]{2,1,0:T(8,128)(2,1)S(1)}, f32[8,128]{1,0:T(8,128)S(1)}) custom-call(s32[2]{0:T(128)S(1)} %copy-done.5, bf16[2,32,1024]{2,1,0:T(8,128)(2,1)S(1)} %copy-done.2, f32[8,256]{1,0:T(8,128)S(1)} %fusion.anch_ref, s32[2,2,256]{2,1,0:T(2,128)S(1)} %copy-done.3, s32[2,1]{1,0:T(2,128)S(1)} %copy.23.cnt_ref, ...), custom_call_target="tpu_custom_call" | custom-call | tf_op jit(solution)/shard_map/exchange/pallas_call | solution.py:212
  30.8 0.0 copy-start
  30.8 0.7 copy-done
  31.5 0.0 copy-start.1
  31.5 0.7 copy-done.1
  32.2 49.7 %work.1 = (bf16[2,81,8,256]{3,2,1,0:T(8,128)(2,1)}, f32[2,16,512]{2,1,0:T(8,128)}) custom-call(s32[1]{0:T(128)} %bitcast.tk_ref, bf16[2,96,1024]{2,1,0:T(8,128)(2,1)} %copy-done, bf16[2,64,1024]{2,1,0:T(8,128)(2,1)} %copy-done.1, s32[2,2,16,512]{3,2,1,0:T(8,128)} %sh_ref.1, f32[2,2,16,512]{3,2,1,0:T(8,128)} %fr_ref.1, bf16[64,16]{1,0:T(8,128)(2,1)} %copy.24.w1_ref, ...), custom_call_target="tpu_custom_call" | custom-call | tf_op jit(solution)/shard_map/work/pallas_call | solution.py:418
  81.9 0.6 slice.15
  (6 shorter events, 0.0 us)
Async XLA Ops:
  7.6 0.9 %copy-start.2 = (bf16[2,32,1024]{2,1,0:T(8,128)(2,1)S(1)}, bf16[2,32,1024]{2,1,0:T(8,128)(2,1)}, u32[]{:S(2)}) copy-start(bf16[2,32,1024]{2,1,0:T(8,128)(2,1)} %img_ref.1) | copy-start | bytes 393220
  8.5 0.7 copy-start.3
  9.2 0.7 copy-start.4
  9.9 0.7 copy-start.5
  30.8 0.7 copy-start
  31.5 0.7 copy-start.1

commit v2 on v1

v2 whole, which is shorter than its diff:
```python
import jax
import jax.numpy as jnp
import numpy as np
from jax import lax
from jax.experimental import pallas as pl
from jax.experimental.pallas import tpu as pltpu
from jax.sharding import PartitionSpec as P

BF = jnp.bfloat16
F32 = jnp.float32
MESH = pl.DeviceIdType.MESH
BIG = -1e30
VMEM_BYTES = 56 * 1024 * 1024

PT = 132
QUADS = PT // 4


def _tables():
    lane = np.arange(128)
    a, b, xx, yy = lane // 64, (lane // 32) % 2, (lane // 16) % 2, lane % 16
    x4, y2 = 2 * xx + b, 2 * yy + a
    ep = np.zeros((4, 96, 6, 128), np.float32)
    for p in range(6):
        ep[x4, 2 * y2 + 15 + p, p, lane] = 1
    oa, ob, ox, oy = lane // 64, (lane // 32) % 2, (lane // 8) % 4, lane % 8
    x8, y1 = 2 * ox + ob, 2 * oy + oa
    eo = np.zeros((8, 64, 6, 128), np.float32)
    for p in range(6):
        eo[x8, 2 * y1 + 15 + p, p, lane] = 1
    wsel = np.zeros((2, 2, 2, 16, 112), np.float32)
    wconst = np.zeros((2, 2, 2, 1, 112), np.float32)
    for e in range(2):
        for ta in range(2):
            for tb in range(2):
                for u in range(4):
                    for v in range(4):
                        wsel[e, ta, tb, 4 * u + v, (u + 2 * ta) * 16 + 8 * e + 2 * tb + v] = 1
                wconst[e, ta, tb, 0, 96 + 4 * e + 2 * ta + tb] = BIG
    extra = np.zeros((3, 3, 16, 256), np.float32)
    cmask = np.zeros((3, 3, 8, 128), np.float32)
    for tk in range(3):
        for gk, g in enumerate((0, 1, QUADS - 1)):
            for half in range(2):
                for e in range(2):
                    for ta in range(2):
                        for tb in range(2):
                            col = 4 * (4 * g + 2 * half + e) - 8 + x4 + tb
                            row = y2 - 8 + ta
                            bad = (col < 0) | (col > 511)
                            if tk == 0:
                                bad = bad | (row < 0)
                            if tk == 2:
                                bad = bad | (row > 15)
                            extra[tk, gk, 4 * e + 2 * ta + tb, 128 * half : 128 * half + 128] = bad
            extra[tk, gk, 8:11] = 1
            ccol, crow = 8 * g - 4 + lane // 16, lane % 16 - 4
            bad = (ccol < 0) | (ccol > 255)
            if tk == 0:
                bad = bad | (crow < 0)
            if tk == 2:
                bad = bad | (crow > 7)
            cmask[tk, gk] = np.where(bad, BIG, 0.0)
    src = np.arange(1024)
    unflat = np.zeros((1024, 1024), np.float32)
    unflat[src, (src % 8) * 128 + src // 8] = 1
    l2 = np.arange(256)
    lx = 8 * (l2 // 128) + 2 * ((l2 // 8) % 4) + (l2 // 32) % 2
    ly = 2 * (l2 % 8) + (l2 // 64) % 2
    perm = np.zeros((256, 256), np.float32)
    perm[16 * lx + ly, l2] = 1
    home = np.stack([ly + 8, lx + 4]).astype(np.float32)
    return dict(
        ep=ep.reshape(384, 768),
        eo=eo.reshape(512, 768),
        wsel=wsel.reshape(8, 16, 112),
        wconst=wconst.reshape(8, 1, 112),
        extra=extra,
        cmask=cmask,
        unflat=unflat,
        home=home,
        perm=perm,
    )


def _split3(x):
    hi = x.astype(BF)
    rest = x - hi.astype(F32)
    mid = rest.astype(BF)
    low = (rest - mid.astype(F32)).astype(BF)
    return hi, mid, low


def _dot(x, y):
    return jnp.dot(x, y, preferred_element_type=F32)


def _kernel(
    pr_ref, cnt_ref, img_ref, sh_ref, fr_ref, ends_ref, stiff_ref, w1_ref, b1_ref, w2_ref, b2_ref,
    wsel_ref, wconst_ref, extra_ref, cmask_ref, home_ref, perm_ref, ep_hbm, eo_hbm, unflat_hbm,
    corr_ref, mis_ref, force_ref,
    j_ref, i_ref, rbuf, anch, gbuf, pbuf, pstage, ep_ref, eo_ref, unflat_ref,
    pad, qp, qo, p4, cpt, obuf, cbuf, wq, bias2, tbuf, px, mpx, fown, cown,
    send_sem, recv_sem, load_sem,
):
    sec = lax.axis_index("sec")
    tile = lax.axis_index("tile")
    back1 = lax.rem(sec + 15, 16)
    back2 = lax.rem(sec + 14, 16)
    fwd1 = lax.rem(sec + 1, 16)
    fwd2 = lax.rem(sec + 2, 16)
    peers = [lax.rem(tile + r, 8) for r in range(8)]
    has_down = tile < 7
    has_up = tile > 0
    tk = jnp.where(tile == 0, 0, jnp.where(tile == 7, 2, 1))

    barrier = pltpu.get_barrier_semaphore()
    for other in (back1, back2, fwd1, fwd2):
        pl.semaphore_signal(barrier, inc=1, device_id=(other, tile), device_id_type=MESH)
    for r in range(1, 8):
        pl.semaphore_signal(barrier, inc=1, device_id=(sec, peers[r]), device_id_type=MESH)

    loads = [
        pltpu.make_async_copy(src, dst, load_sem.at[k])
        for k, (src, dst) in enumerate(((eo_hbm, eo_ref), (ep_hbm, ep_ref), (unflat_hbm, unflat_ref)))
    ]
    for c in loads:
        c.start()

    rows = [sh_ref[s, k, 0:1, :].astype(F32) + fr_ref[s, k, 0:1, :] for s in range(2) for k in range(2)]
    rows = jnp.concatenate(rows + [jnp.zeros((4, 512), F32)], axis=0)
    x_at = lax.broadcasted_iota(jnp.int32, (512, 256), 0)
    v_at = lax.broadcasted_iota(jnp.int32, (512, 256), 1)
    select = jnp.where(x_at == 16 * (v_at - 32 * tile), 1.0, 0.0).astype(BF)
    got = _dot(jnp.concatenate(_split3(rows), axis=0).astype(BF), select)
    anch[...] = (got[16:24] + got[8:16]) + got[0:8]

    pl.semaphore_wait(barrier, 11)

    def remote(src, dst, k, target):
        return pltpu.make_async_remote_copy(
            src_ref=src, dst_ref=dst, send_sem=send_sem.at[k], recv_sem=recv_sem.at[k],
            device_id=target, device_id_type=MESH,
        )

    near = remote(img_ref, rbuf.at[0], 0, (back1, tile))
    far = remote(img_ref, rbuf.at[1], 1, (back2, tile))
    far.start()
    near.start()
    down_tile = (sec, lax.rem(tile + 1, 8))
    up_tile = (sec, lax.rem(tile + 7, 8))
    own_down = remote(img_ref.at[:, 16:32], i_ref.at[:, 0:16], 2, down_tile)
    own_up = remote(img_ref.at[:, 0:16], i_ref.at[:, 48:64], 3, up_tile)
    pl.when(has_down)(own_down.start)
    pl.when(has_up)(own_up.start)
    anchor_sends = [remote(anch, gbuf.at[r], 4 + r, (sec, peers[r])) for r in range(1, 8)]
    for c in anchor_sends:
        c.start()

    i_ref[:, 16:48, :] = img_ref[...]

    @pl.when(tile == 0)
    def _():
        i_ref[:, 0:16, :] = jnp.zeros((2, 16, 1024), BF)
        j_ref[:, 0:32, :] = jnp.zeros((2, 32, 1024), BF)

    @pl.when(tile == 7)
    def _():
        i_ref[:, 48:64, :] = jnp.zeros((2, 16, 1024), BF)
        j_ref[:, 64:96, :] = jnp.zeros((2, 32, 1024), BF)

    lane = lax.broadcasted_iota(jnp.int32, (64, 112), 1)
    bias1 = jnp.broadcast_to(b1_ref[...], (128, 64)).T[:, 0:112]
    hi, mid, low = (x.astype(F32) for x in _split3(bias1))
    base = (
        jnp.where(lane == 104, hi, 0.0) + jnp.where(lane == 105, mid, 0.0) + jnp.where(lane == 106, low, 0.0)
    )
    for m in range(8):
        spread = lax.dot_general(
            w1_ref[...], wsel_ref[m], (((0,), (0,)), ((), ())), preferred_element_type=F32
        )
        wq[64 * m : 64 * m + 64, :] = (spread + base + wconst_ref[m]).astype(BF)
    bias2[...] = jnp.broadcast_to(b2_ref[...], (128, 64)).T

    lane128 = lax.broadcasted_iota(jnp.int32, (1, 128), 1)
    x_bit = [lax.bitwise_and(lax.shift_right_logical(lane128, 3 + k), 1) == 1 for k in range(4)]
    y_bit = [lax.bitwise_and(lax.shift_right_logical(lane128, k), 1) == 1 for k in range(3)]
    row16 = lax.broadcasted_iota(jnp.int32, (16, 256), 0)

    def pixels(s, carry):
        planes = [sh_ref[s, k].astype(F32) for k in range(2)] + [fr_ref[s, k] for k in range(2)]
        tbuf[:, 0:64] = jnp.concatenate(planes, axis=0).T
        runs = [tbuf[pl.ds(x, 32, stride=16), :] for x in range(16)]
        planes = [jnp.concatenate([r[:, 16 * k : 16 * k + 16] for r in runs], axis=1) for k in range(4)]
        parts = [planes[0].astype(BF), planes[1].astype(BF), *_split3(planes[2]), *_split3(planes[3])]
        got = _dot(jnp.concatenate(parts, axis=0), perm_ref[...])
        px[s, 0] = got[0:32] + home_ref[0:1, :]
        px[s, 1] = got[32:64] + home_ref[1:2, :]
        px[s, 2] = (got[128:160] + got[96:128]) + got[64:96]
        px[s, 3] = (got[224:256] + got[192:224]) + got[160:192]
        return carry

    lax.fori_loop(0, 2, pixels, 0)

    for c in anchor_sends:
        c.wait()
    disp = anch[...]
    for r in range(1, 8):
        disp = disp + gbuf[r]
    vert = lax.broadcasted_iota(jnp.int32, (256, 256), 0)
    slot_at = lax.broadcasted_iota(jnp.int32, (1, 256), 1)
    row_of = lax.broadcasted_iota(jnp.int32, (8, 256), 0)
    parts = jnp.concatenate(_split3(disp), axis=0)
    total = jnp.zeros((8, 256), F32)
    for s in range(2):
        table = (vert == ends_ref[s, 1:2, :]).astype(F32) - (vert == ends_ref[s, 0:1, :]).astype(F32)
        table = table.astype(BF)
        got = _dot(parts, table)
        spread = (got[16:24] + got[8:16]) + got[0:8]
        pull = jnp.where(slot_at < cnt_ref[0, s], stiff_ref[s : s + 1, :], 0.0) * spread
        back = lax.dot_general(
            jnp.concatenate(_split3(pull), axis=0), table, (((1,), (1,)), ((), ())),
            preferred_element_type=F32,
        )
        back = (back[16:24] + back[8:16]) + back[0:8]
        total = total - jnp.where(lax.shift_right_logical(row_of, 1) == s, back, 0.0)
    pstage[...] = total
    force_sends = [remote(pstage, pbuf.at[r], 14 + r, (sec, peers[r])) for r in range(1, 8)]
    for c in force_sends:
        c.start()

    near.wait()
    far.wait()
    for s in range(2):
        p = pr_ref[s]
        which = jnp.where(lax.shift_right_logical(p, 1) == fwd1, 0, 1)
        slot = lax.bitwise_and(p, 1)
        j_ref[s, 32:64, :] = rbuf[which, slot]
    part_down = remote(j_ref.at[:, 32:64], j_ref.at[:, 0:32], 12, down_tile)
    part_up = remote(j_ref.at[:, 32:64], j_ref.at[:, 64:96], 13, up_tile)
    pl.when(has_down)(part_down.start)
    pl.when(has_up)(part_up.start)

    pl.when(has_down)(own_down.wait_send)
    pl.when(has_up)(own_up.wait_send)
    pl.when(has_up)(own_down.wait_recv)
    pl.when(has_down)(own_up.wait_recv)
    loads[0].wait()

    def side_by_side(left, right, more):
        return jnp.concatenate(
            [
                jnp.concatenate([left[:, 128 * p : 128 * p + 128], right[:, 128 * p : 128 * p + 128]], axis=1)
                for p in range(6)
            ]
            + [more],
            axis=0,
        )

    def own(s, carry):
        pad[0:64, 0:1024] = i_ref[s].astype(F32)
        pad[0:96, 1024:1152] = jnp.zeros((96, 128), F32)
        wide = pad[0:64, :]
        stack = jnp.concatenate(
            [pltpu.roll(wide, (1 - 2 * k) % 1152, 1)[:, 0:1024] for k in range(8)], axis=0
        )
        qo[...] = _dot(stack.T.astype(BF), eo_ref[...]).astype(BF)

        def encode(c, carry):
            small = []
            for n in range(4):
                r0 = pl.multiple_of(128 * c + 32 * n, 32)
                patches = side_by_side(qo[pl.ds(r0, 16), :], qo[pl.ds(r0 + 16, 16), :], extra_ref[1, 1])
                own4 = jnp.maximum(_dot(wq[0:256, :], patches).astype(BF), 0)
                fown[s, :, pl.ds(pl.multiple_of(1024 * c + 256 * n, 256), 256)] = own4[0:64, :]
                small += [own4[:, 0:32], own4[:, 128:160]]
            pre = _dot(w2_ref[...], jnp.concatenate(small, axis=1))
            pre = jnp.maximum(pre + jnp.concatenate([bias2[...]] * 2, axis=1), 0.0)
            cown[s, :, pl.ds(pl.multiple_of(256 * c, 256), 256)] = pre.astype(BF)
            return carry

        return lax.fori_loop(0, 8, encode, carry)

    lax.fori_loop(0, 2, own, 0)

    for c in force_sends:
        c.wait()
    total = pstage[...]
    for r in range(1, 8):
        total = total + pbuf[r]
    turned = pltpu.roll(total, lax.rem(256 - 32 * tile, 256), 1)
    for s in range(2):
        force_ref[s] = turned[2 * s : 2 * s + 2, 0:32]

    pl.when(has_down)(part_down.wait_send)
    pl.when(has_up)(part_up.wait_send)
    pl.when(has_up)(part_down.wait_recv)
    pl.when(has_down)(part_up.wait_recv)
    loads[1].wait()
    loads[2].wait()

    def section(s, carry):
        pad[0:96, 0:1024] = j_ref[s].astype(F32)
        wide = pad[...]
        stack = jnp.concatenate([pltpu.roll(wide, (17 - 2 * k) % 1152, 1) for k in range(4)], axis=0)
        qp[...] = _dot(stack.T.astype(BF), ep_ref[...])[0:1056].astype(BF)

        def partner(g, carry):
            r0 = pl.multiple_of(32 * g, 32)
            kind = jnp.where(g == 0, 0, jnp.where(g == QUADS - 1, 2, 1))
            patches = side_by_side(qp[pl.ds(r0, 16), :], qp[pl.ds(r0 + 16, 16), :], extra_ref[tk, kind])
            got = jnp.maximum(_dot(wq[...], patches).astype(BF), 0)
            l0 = pl.multiple_of(512 * g, 512)
            p4[:, pl.ds(l0, 512)] = jnp.concatenate(
                [got[0:256, 0:128], got[256:512, 0:128], got[0:256, 128:256], got[256:512, 128:256]], axis=1
            )
            return carry

        lax.fori_loop(0, QUADS, partner, 0, unroll=3)

        def coarsen(q, count):
            tiles = p4[:, pl.ds(pl.multiple_of(512 * q, 512), 512 * count)]
            tiles = jnp.concatenate([tiles[:, 128 * k : 128 * k + 32] for k in range(4 * count)], axis=1)
            pre = _dot(w2_ref[...], tiles)
            for n in range(count):
                kind = jnp.where(q + n == 0, 0, jnp.where(q + n == QUADS - 1, 2, 1))
                coarse = pre[:, 128 * n : 128 * n + 128] + bias2[...] + cmask_ref[tk, kind][0:1, :]
                coarse = jnp.maximum(coarse, 0.0).astype(BF).astype(F32)
                cpt[pl.ds(pl.multiple_of(128 * (q + n), 128), 128), 0:64] = coarse.T.astype(BF)

        def coarsen_four(g, carry):
            coarsen(4 * g, 4)
            return carry

        lax.fori_loop(0, QUADS // 4, coarsen_four, 0, unroll=2)
        coarsen(QUADS - 1, 1)

        def block(c, carry):
            for half in range(2):
                b = 2 * c + half
                own_map = fown[s, :, pl.ds(pl.multiple_of(256 * b, 256), 256)].astype(F32)
                row = px[s, 0, pl.ds(b, 1), :]
                col = px[s, 1, pl.ds(b, 1), :]
                fy = px[s, 2, pl.ds(b, 1), :]
                fx = px[s, 3, pl.ds(b, 1), :]
                row = jnp.broadcast_to(row.astype(jnp.int32), (16, 256))
                col = jnp.broadcast_to(col, (16, 256)).astype(BF)
                oy = [(row == 2 * row16 + a).astype(F32).astype(BF) for a in range(2)]
                zero = jnp.zeros((16, 256), BF)
                picks = []
                for k in range(6):
                    hit = {}
                    for bb in range(2):
                        for xx in range(2):
                            hit[bb, xx] = col == float(4 * k + 2 * xx + bb)
                    for a in range(2):
                        for bb in range(2):
                            for xx in range(2):
                                picks.append(jnp.where(hit[bb, xx], oy[a], zero))
                choose = jnp.concatenate(picks, axis=0)
                l0 = pl.multiple_of(512 * b + 128, 128)
                taps = _dot(p4[:, pl.ds(l0, 768)], choose)
                gy, gx = 1.0 - fy, 1.0 - fx
                warped = (
                    (gy * gx) * taps[0:64] + (gy * fx) * taps[64:128]
                    + (fy * gx) * taps[128:192] + (fy * fx) * taps[192:256]
                )
                differ = own_map - warped
                mpx[pl.ds(b, 1), :] = jnp.sum(differ * differ, axis=0, keepdims=True) * (1.0 / 64)

            coarse = cown[s, :, pl.ds(pl.multiple_of(128 * c, 128), 128)]
            there = cpt[pl.ds(pl.multiple_of(256 * c, 256), 384), 0:64]
            gram = _dot(there, coarse).reshape(24, 16, 128)
            for k, keep in ((3, 16), (2, 12), (1, 10), (0, 9)):
                step = 1 << k
                gram = jnp.where(x_bit[k][None], gram[step : step + keep], gram[0:keep])
            gram = gram.reshape(144, 128)
            cols = []
            for j in range(9):
                v = gram[16 * j : 16 * j + 16]
                for k in (2, 1, 0):
                    v = jnp.where(y_bit[k], pltpu.roll(v, 16 - (1 << k), 0), v)
                cols.append(v)
            gram = jnp.concatenate(cols, axis=0) * (1.0 / 64)
            obuf[:, pl.ds(pl.multiple_of(128 * c, 128), 128)] = gram.astype(BF)
            return carry

        lax.fori_loop(0, 16, block, 0)

        got = lax.dot_general(
            jnp.concatenate(_split3(mpx[...]), axis=0), perm_ref[...], (((1,), (1,)), ((), ())),
            preferred_element_type=F32,
        )
        got = (got[64:96] + got[32:64]) + got[0:32]
        for x in range(16):
            tbuf[pl.ds(x, 32, stride=16), 0:16] = got[:, 16 * x : 16 * x + 16]
        mis_ref[s] = tbuf[...].T[0:16, :]

        for h in range(2):
            flat = _dot(obuf[:, 1024 * h : 1024 * h + 1024], unflat_ref[...])
            for j in range(9):
                for y in range(8):
                    cbuf[h, pl.ds(8 * j + y, 9, stride=72), :] = flat[16 * j : 16 * j + 9, 128 * y : 128 * y + 128]
        for h in range(2):
            corr_ref[s, :, :, 128 * h : 128 * h + 128] = cbuf[h].reshape(81, 8, 128).astype(BF)
        return carry

    lax.fori_loop(0, 2, section, 0)


def local(
    section_image, partner_row, base_shift, bilinear_frac, first_kernel, initial_conv_bias,
    second_kernel, second_bias, edge_ends, edge_count, stiffness,
):
    t = _tables()
    vm = pl.BlockSpec(memory_space=pltpu.VMEM)
    sm = pl.BlockSpec(memory_space=pltpu.SMEM)
    hbm = pl.BlockSpec(memory_space=pl.ANY)
    consts = [
        jnp.asarray(t["wsel"], BF), jnp.asarray(t["wconst"], F32), jnp.asarray(t["extra"], BF),
        jnp.asarray(t["cmask"], F32), jnp.asarray(t["home"], F32), jnp.asarray(t["perm"], BF),
        jnp.asarray(t["ep"], BF), jnp.asarray(t["eo"], BF), jnp.asarray(t["unflat"], BF),
    ]
    return pl.pallas_call(
        _kernel,
        out_shape=(
            jax.ShapeDtypeStruct((2, 81, 8, 256), BF),
            jax.ShapeDtypeStruct((2, 16, 512), F32),
            jax.ShapeDtypeStruct((2, 2, 32), F32),
        ),
        in_specs=[sm, sm] + [vm] * 15 + [hbm] * 3,
        out_specs=(vm, vm, vm),
        scratch_shapes=[
            pltpu.VMEM((2, 96, 1024), BF),
            pltpu.VMEM((2, 64, 1024), BF),
            pltpu.VMEM((2, 2, 32, 1024), BF),
            pltpu.VMEM((8, 256), F32),
            pltpu.VMEM((8, 8, 256), F32),
            pltpu.VMEM((8, 8, 256), F32),
            pltpu.VMEM((8, 256), F32),
            pltpu.VMEM((384, 768), BF),
            pltpu.VMEM((512, 768), BF),
            pltpu.VMEM((1024, 1024), BF),
            pltpu.VMEM((96, 1152), F32),
            pltpu.VMEM((1056, 768), BF),
            pltpu.VMEM((1024, 768), BF),
            pltpu.VMEM((256, PT * 128), BF),
            pltpu.VMEM((PT * 32, 128), BF),
            pltpu.VMEM((144, 2048), BF),
            pltpu.VMEM((2, 648, 128), F32),
            pltpu.VMEM((512, 112), BF),
            pltpu.VMEM((64, 128), F32),
            pltpu.VMEM((512, 128), F32),
            pltpu.VMEM((2, 4, 32, 256), F32),
            pltpu.VMEM((32, 256), F32),
            pltpu.VMEM((2, 64, 8192), BF),
            pltpu.VMEM((2, 64, 2048), BF),
            pltpu.SemaphoreType.DMA((22,)),
            pltpu.SemaphoreType.DMA((22,)),
            pltpu.SemaphoreType.DMA((3,)),
        ],
        compiler_params=pltpu.CompilerParams(
            collective_id=0, has_side_effects=True, vmem_limit_bytes=VMEM_BYTES
        ),
        name="align",
    )(
        partner_row, edge_count.T, section_image, base_shift, bilinear_frac, edge_ends, stiffness,
        first_kernel.T, initial_conv_bias.reshape(1, 64), second_kernel, second_bias.reshape(1, 64), *consts,
    )


def solution(mesh):
    in_specs = (
        P("sec", "tile", None), P("sec"), P("sec", None, "tile", None), P("sec", None, "tile", None),
        P(), P(), P(), P(), P("sec", None, "tile"), P("sec", "tile"), P("sec", "tile"),
    )
    out_specs = (P("sec", None, "tile", None), P("sec", "tile", None), P("sec", None, "tile"))
    return jax.shard_map(local, mesh=mesh, in_specs=in_specs, out_specs=out_specs, check_vma=False)
```

time: 82.9 us -> 68.4 us (0.83)
  the two profiles are of different devices: /device:TPU:15 before, /device:TPU:7 now
where the time goes in v2:
time: 68.4 us; the launch traced here: 68.1 us
  Pallas kernels  62.8 us (92%)
  local copies, waits for them, and re-layouts  4.69 us (7%)
    pallas_call x1, Pallas kernels, local(): pl.pallas_call(_kernel, out_shape=(jax.ShapeDtypeStruct((2, 81, 8, 256),...  62.8 us
    unnamed x3, local copies, waits for them, and re-layouts  4.69 us

profile of v2, /device:TPU:7, one launch (start us, length us, event | category | flops | bytes accessed | tf_op | source)
XLA Modules:
  0.0 68.1 jit_solution(16442420467932164861)
XLA Ops:
  0.6 62.8 %align.1 = (bf16[2,81,8,256]{3,2,1,0:T(8,128)(2,1)}, f32[2,16,512]{2,1,0:T(8,128)}, f32[2,2,32]{2,1,0:T(2,128)}) custom-call(s32[2]{0:T(128)} %pr_ref.1, s32[1,2]{1,0:T(1,128)} %bitcast.5, bf16[2,32,1024]{2,1,0:T(8,128)(2,1)} %img_ref.1, s32[2,2,16,512]{3,2,1,0:T(8,128)} %sh_ref.1, f32[2,2,16,512]{3,2,1,0:T(8,128)} %fr_ref.1, s32[2,2,256]{2,1,0:T(2,128)} %ends_ref.1, ...), custom_call_target="tpu_custom_call" | custom-call | tf_op jit(solution)/shard_map/align/pallas_call | solution.py:424
  63.4 2.0 %copy.26 = bf16[2,81,8,256]{3,2,1,0:T(8,128)(2,1)} copy(bf16[2,81,8,256]{3,2,1,0:T(8,128)(2,1)} %get-tuple-element.6) | data formatting | bytes 1327104
  65.4 1.5 %copy.27 = f32[2,16,512]{2,1,0:T(8,128)} copy(f32[2,16,512]{2,1,0:T(8,128)} %get-tuple-element.7) | data formatting | bytes 131072
  66.9 1.2 %copy.28 = f32[2,2,32]{2,1,0:T(2,128)} copy(f32[2,2,32]{2,1,0:T(2,128)} %get-tuple-element.8) | data formatting | bytes 1024

commit v3 on v2

--- a/solution.py
+++ b/solution.py
@@ -135,6 +135,39 @@
     got = _dot(jnp.concatenate(_split3(rows), axis=0).astype(BF), select)
     anch[...] = (got[16:24] + got[8:16]) + got[0:8]
 
+    lane = lax.broadcasted_iota(jnp.int32, (64, 112), 1)
+    bias1 = jnp.broadcast_to(b1_ref[...], (128, 64)).T[:, 0:112]
+    hi, mid, low = (x.astype(F32) for x in _split3(bias1))
+    base = (
+        jnp.where(lane == 104, hi, 0.0) + jnp.where(lane == 105, mid, 0.0) + jnp.where(lane == 106, low, 0.0)
+    )
+    for m in range(8):
+        spread = lax.dot_general(
+            w1_ref[...], wsel_ref[m], (((0,), (0,)), ((), ())), preferred_element_type=F32
+        )
+        wq[64 * m : 64 * m + 64, :] = (spread + base + wconst_ref[m]).astype(BF)
+    bias2[...] = jnp.broadcast_to(b2_ref[...], (128, 64)).T
+
+    lane128 = lax.broadcasted_iota(jnp.int32, (1, 128), 1)
+    x_bit = [lax.bitwise_and(lax.shift_right_logical(lane128, 3 + k), 1) == 1 for k in range(4)]
+    y_bit = [lax.bitwise_and(lax.shift_right_logical(lane128, k), 1) == 1 for k in range(3)]
+    row16 = lax.broadcasted_iota(jnp.int32, (16, 256), 0)
+
+    def pixels(s, carry):
+        planes = [sh_ref[s, k].astype(F32) for k in range(2)] + [fr_ref[s, k] for k in range(2)]
+        tbuf[:, 0:64] = jnp.concatenate(planes, axis=0).T
+        runs = [tbuf[pl.ds(x, 32, stride=16), :] for x in range(16)]
+        planes = [jnp.concatenate([r[:, 16 * k : 16 * k + 16] for r in runs], axis=1) for k in range(4)]
+        parts = [planes[0].astype(BF), planes[1].astype(BF), *_split3(planes[2]), *_split3(planes[3])]
+        got = _dot(jnp.concatenate(parts, axis=0), perm_ref[...])
+        px[s, 0] = got[0:32] + home_ref[0:1, :]
+        px[s, 1] = got[32:64] + home_ref[1:2, :]
+        px[s, 2] = (got[128:160] + got[96:128]) + got[64:96]
+        px[s, 3] = (got[224:256] + got[192:224]) + got[160:192]
+        return carry
+
+    lax.fori_loop(0, 2, pixels, 0)
+
     pl.semaphore_wait(barrier, 11)
 
     def remote(src, dst, k, target):
@@ -168,39 +201,6 @@
     def _():
         i_ref[:, 48:64, :] = jnp.zeros((2, 16, 1024), BF)
         j_ref[:, 64:96, :] = jnp.zeros((2, 32, 1024), BF)
-
-    lane = lax.broadcasted_iota(jnp.int32, (64, 112), 1)
-    bias1 = jnp.broadcast_to(b1_ref[...], (128, 64)).T[:, 0:112]
-    hi, mid, low = (x.astype(F32) for x in _split3(bias1))
-    base = (
-        jnp.where(lane == 104, hi, 0.0) + jnp.where(lane == 105, mid, 0.0) + jnp.where(lane == 106, low, 0.0)
-    )
-    for m in range(8):
-        spread = lax.dot_general(
-            w1_ref[...], wsel_ref[m], (((0,), (0,)), ((), ())), preferred_element_type=F32
-        )
-        wq[64 * m : 64 * m + 64, :] = (spread + base + wconst_ref[m]).astype(BF)
-    bias2[...] = jnp.broadcast_to(b2_ref[...], (128, 64)).T
-
-    lane128 = lax.broadcasted_iota(jnp.int32, (1, 128), 1)
-    x_bit = [lax.bitwise_and(lax.shift_right_logical(lane128, 3 + k), 1) == 1 for k in range(4)]
-    y_bit = [lax.bitwise_and(lax.shift_right_logical(lane128, k), 1) == 1 for k in range(3)]
-    row16 = lax.broadcasted_iota(jnp.int32, (16, 256), 0)
-
-    def pixels(s, carry):
-        planes = [sh_ref[s, k].astype(F32) for k in range(2)] + [fr_ref[s, k] for k in range(2)]
-        tbuf[:, 0:64] = jnp.concatenate(planes, axis=0).T
-        runs = [tbuf[pl.ds(x, 32, stride=16), :] for x in range(16)]
-        planes = [jnp.concatenate([r[:, 16 * k : 16 * k + 16] for r in runs], axis=1) for k in range(4)]
-        parts = [planes[0].astype(BF), planes[1].astype(BF), *_split3(planes[2]), *_split3(planes[3])]
-        got = _dot(jnp.concatenate(parts, axis=0), perm_ref[...])
-        px[s, 0] = got[0:32] + home_ref[0:1, :]
-        px[s, 1] = got[32:64] + home_ref[1:2, :]
-        px[s, 2] = (got[128:160] + got[96:128]) + got[64:96]
-        px[s, 3] = (got[224:256] + got[192:224]) + got[160:192]
-        return carry
-
-    lax.fori_loop(0, 2, pixels, 0)
 
     for c in anchor_sends:
         c.wait()
@@ -229,18 +229,6 @@
     for c in force_sends:
         c.start()
 
-    near.wait()
-    far.wait()
-    for s in range(2):
-        p = pr_ref[s]
-        which = jnp.where(lax.shift_right_logical(p, 1) == fwd1, 0, 1)
-        slot = lax.bitwise_and(p, 1)
-        j_ref[s, 32:64, :] = rbuf[which, slot]
-    part_down = remote(j_ref.at[:, 32:64], j_ref.at[:, 0:32], 12, down_tile)
-    part_up = remote(j_ref.at[:, 32:64], j_ref.at[:, 64:96], 13, up_tile)
-    pl.when(has_down)(part_down.start)
-    pl.when(has_up)(part_up.start)
-
     pl.when(has_down)(own_down.wait_send)
     pl.when(has_up)(own_up.wait_send)
     pl.when(has_up)(own_down.wait_recv)
@@ -279,9 +267,23 @@
             cown[s, :, pl.ds(pl.multiple_of(256 * c, 256), 256)] = pre.astype(BF)
             return carry
 
-        return lax.fori_loop(0, 8, encode, carry)
-
-    lax.fori_loop(0, 2, own, 0)
+        return lax.fori_loop(0, 8, encode, carry, unroll=4)
+
+    own(0, 0)
+
+    near.wait()
+    far.wait()
+    for s in range(2):
+        p = pr_ref[s]
+        which = jnp.where(lax.shift_right_logical(p, 1) == fwd1, 0, 1)
+        slot = lax.bitwise_and(p, 1)
+        j_ref[s, 32:64, :] = rbuf[which, slot]
+    part_down = remote(j_ref.at[:, 32:64], j_ref.at[:, 0:32], 12, down_tile)
+    part_up = remote(j_ref.at[:, 32:64], j_ref.at[:, 64:96], 13, up_tile)
+    pl.when(has_down)(part_down.start)
+    pl.when(has_up)(part_up.start)
+
+    own(1, 0)
 
     for c in force_sends:
         c.wait()
@@ -316,8 +318,6 @@
             )
             return carry
 
-        lax.fori_loop(0, QUADS, partner, 0, unroll=3)
-
         def coarsen(q, count):
             tiles = p4[:, pl.ds(pl.multiple_of(512 * q, 512), 512 * count)]
             tiles = jnp.concatenate([tiles[:, 128 * k : 128 * k + 32] for k in range(4 * count)], axis=1)
@@ -328,11 +328,17 @@
                 coarse = jnp.maximum(coarse, 0.0).astype(BF).astype(F32)
                 cpt[pl.ds(pl.multiple_of(128 * (q + n), 128), 128), 0:64] = coarse.T.astype(BF)
 
-        def coarsen_four(g, carry):
-            coarsen(4 * g, 4)
+        def both(g, carry):
+            coarsen(4 * g - 4, 4)
+            for n in range(4):
+                partner(4 * g + n, carry)
             return carry
 
-        lax.fori_loop(0, QUADS // 4, coarsen_four, 0, unroll=2)
+        for n in range(4):
+            partner(n, 0)
+        lax.fori_loop(1, QUADS // 4, both, 0)
+        coarsen(QUADS - 5, 4)
+        partner(QUADS - 1, 0)
         coarsen(QUADS - 1, 1)
 
         def block(c, carry):
@@ -382,10 +388,10 @@
                     v = jnp.where(y_bit[k], pltpu.roll(v, 16 - (1 << k), 0), v)
                 cols.append(v)
             gram = jnp.concatenate(cols, axis=0) * (1.0 / 64)
-            obuf[:, pl.ds(pl.multiple_of(128 * c, 128), 128)] = gram.astype(BF)
+            obuf[pl.ds(pl.multiple_of(144 * s, 16), 144), pl.ds(pl.multiple_of(128 * c, 128), 128)] = gram.astype(BF)
             return carry
 
-        lax.fori_loop(0, 16, block, 0)
+        lax.fori_loop(0, 16, block, 0, unroll=2)
 
         got = lax.dot_general(
             jnp.concatenate(_split3(mpx[...]), axis=0), perm_ref[...], (((1,), (1,)), ((), ())),
@@ -396,16 +402,25 @@
             tbuf[pl.ds(x, 32, stride=16), 0:16] = got[:, 16 * x : 16 * x + 16]
         mis_ref[s] = tbuf[...].T[0:16, :]
 
-        for h in range(2):
-            flat = _dot(obuf[:, 1024 * h : 1024 * h + 1024], unflat_ref[...])
+        return carry
+
+    lax.fori_loop(0, 2, section, 0)
+
+    for h in range(2):
+        flat = _dot(obuf[:, 1024 * h : 1024 * h + 1024], unflat_ref[...])
+        for s in range(2):
             for j in range(9):
+                r0 = 144 * s + 16 * j
                 for y in range(8):
-                    cbuf[h, pl.ds(8 * j + y, 9, stride=72), :] = flat[16 * j : 16 * j + 9, 128 * y : 128 * y + 128]
-        for h in range(2):
-            corr_ref[s, :, :, 128 * h : 128 * h + 128] = cbuf[h].reshape(81, 8, 128).astype(BF)
-        return carry
-
-    lax.fori_loop(0, 2, section, 0)
+                    cbuf[s, pl.ds(8 * j + y, 9, stride=72), :] = flat[r0 : r0 + 9, 128 * y : 128 * y + 128]
+        for s in range(2):
+            corr_ref[s, :, :, 128 * h : 128 * h + 128] = cbuf[s].reshape(81, 8, 128).astype(BF)
+
+
+def _hand_on(a, b, c, x, y, z):
+    x[...] = a[...]
+    y[...] = b[...]
+    z[...] = c[...]
 
 
 def local(
@@ -421,7 +436,7 @@
         jnp.asarray(t["cmask"], F32), jnp.asarray(t["home"], F32), jnp.asarray(t["perm"], BF),
         jnp.asarray(t["ep"], BF), jnp.asarray(t["eo"], BF), jnp.asarray(t["unflat"], BF),
     ]
-    return pl.pallas_call(
+    results = pl.pallas_call(
         _kernel,
         out_shape=(
             jax.ShapeDtypeStruct((2, 81, 8, 256), BF),
@@ -446,7 +461,7 @@
             pltpu.VMEM((1024, 768), BF),
             pltpu.VMEM((256, PT * 128), BF),
             pltpu.VMEM((PT * 32, 128), BF),
-            pltpu.VMEM((144, 2048), BF),
+            pltpu.VMEM((288, 2048), BF),
             pltpu.VMEM((2, 648, 128), F32),
             pltpu.VMEM((512, 112), BF),
             pltpu.VMEM((64, 128), F32),
@@ -467,6 +482,13 @@
         partner_row, edge_count.T, section_image, base_shift, bilinear_frac, edge_ends, stiffness,
         first_kernel.T, initial_conv_bias.reshape(1, 64), second_kernel, second_bias.reshape(1, 64), *consts,
     )
+    return pl.pallas_call(
+        _hand_on,
+        out_shape=tuple(jax.ShapeDtypeStruct(r.shape, r.dtype) for r in results),
+        in_specs=[vm] * 3,
+        out_specs=(vm,) * 3,
+        name="hand_on",
+    )(*results)
 
 
 def solution(mesh):

time: 68.4 us -> 56.7 us (0.83)
  the two profiles are of different devices: /device:TPU:7 before, /device:TPU:0 now
where the time goes in v3:
time: 56.7 us; the launch traced here: 56.6 us
  Pallas kernels  55.9 us (99%)
  between operations  0.64 us (1%)
    pallas_call x1, Pallas kernels, local(): pl.pallas_call(_kernel, out_shape=(jax.ShapeDtypeStruct((2, 81, 8, 256),...  53.9 us
    pallas_call x1, Pallas kernels, local(): pl.pallas_call(_hand_on, out_shape=tuple((jax.ShapeDtypeStruct(r.shape, r...  2.02 us

profile of v3, /device:TPU:0, one launch (start us, length us, event | category | flops | bytes accessed | tf_op | source)
XLA Modules:
  0.0 56.6 jit_solution(2340570487920154620)
XLA Ops:
  0.6 53.9 %align.1 = (bf16[2,81,8,256]{3,2,1,0:T(8,128)(2,1)}, f32[2,16,512]{2,1,0:T(8,128)}, f32[2,2,32]{2,1,0:T(2,128)}) custom-call(s32[2]{0:T(128)} %pr_ref.1, s32[1,2]{1,0:T(1,128)} %bitcast.5, bf16[2,32,1024]{2,1,0:T(8,128)(2,1)} %img_ref.1, s32[2,2,16,512]{3,2,1,0:T(8,128)} %sh_ref.1, f32[2,2,16,512]{3,2,1,0:T(8,128)} %fr_ref.1, s32[2,2,256]{2,1,0:T(2,128)} %ends_ref.1, ...), custom_call_target="tpu_custom_call" | custom-call | tf_op jit(solution)/shard_map/align/pallas_call | solution.py:439
  54.5 2.0 %hand_on.1 = (bf16[2,81,8,256]{3,2,1,0:T(8,128)(2,1)}, f32[2,16,512]{2,1,0:T(8,128)}, f32[2,2,32]{2,1,0:T(2,128)}) custom-call(bf16[2,81,8,256]{3,2,1,0:T(8,128)(2,1)} %get-tuple-element.6.a, f32[2,16,512]{2,1,0:T(8,128)} %get-tuple-element.7.b, f32[2,2,32]{2,1,0:T(2,128)} %get-tuple-element.8.c), custom_call_target="tpu_custom_call" | custom-call | tf_op jit(solution)/shard_map/hand_on/pallas_call | solution.py:485

commit v4 on v3

--- a/solution.py
+++ b/solution.py
@@ -20,7 +20,7 @@
     lane = np.arange(128)
     a, b, xx, yy = lane // 64, (lane // 32) % 2, (lane // 16) % 2, lane % 16
     x4, y2 = 2 * xx + b, 2 * yy + a
-    ep = np.zeros((4, 96, 6, 128), np.float32)
+    ep = np.zeros((4, 128, 6, 128), np.float32)
     for p in range(6):
         ep[x4, 2 * y2 + 15 + p, p, lane] = 1
     oa, ob, ox, oy = lane // 64, (lane // 32) % 2, (lane // 8) % 4, lane % 8
@@ -71,7 +71,7 @@
     perm[16 * lx + ly, l2] = 1
     home = np.stack([ly + 8, lx + 4]).astype(np.float32)
     return dict(
-        ep=ep.reshape(384, 768),
+        ep=ep.reshape(512, 768),
         eo=eo.reshape(512, 768),
         wsel=wsel.reshape(8, 16, 112),
         wconst=wconst.reshape(8, 1, 112),
@@ -100,7 +100,7 @@
     wsel_ref, wconst_ref, extra_ref, cmask_ref, home_ref, perm_ref, ep_hbm, eo_hbm, unflat_hbm,
     corr_ref, mis_ref, force_ref,
     j_ref, i_ref, rbuf, anch, gbuf, pbuf, pstage, ep_ref, eo_ref, unflat_ref,
-    pad, qp, qo, p4, cpt, obuf, cbuf, wq, bias2, tbuf, px, mpx, fown, cown,
+    tall, qp, qo, p4, cpt, obuf, cbuf, wq, bias2, tbuf, px, mpx, fown, cown,
     send_sem, recv_sem, load_sem,
 ):
     sec = lax.axis_index("sec")
@@ -246,23 +246,22 @@
         )
 
     def own(s, carry):
-        pad[0:64, 0:1024] = i_ref[s].astype(F32)
-        pad[0:96, 1024:1152] = jnp.zeros((96, 128), F32)
-        wide = pad[0:64, :]
-        stack = jnp.concatenate(
-            [pltpu.roll(wide, (1 - 2 * k) % 1152, 1)[:, 0:1024] for k in range(8)], axis=0
-        )
-        qo[...] = _dot(stack.T.astype(BF), eo_ref[...]).astype(BF)
+        wide = jnp.concatenate([i_ref[s].astype(F32), jnp.zeros((64, 128), F32)], axis=1)
+        turned = jnp.concatenate([pltpu.roll(wide, 1, 1), pltpu.roll(wide, 1151, 1)], axis=0)
+        tall[...] = turned.T
+        stack = jnp.concatenate([tall[4 * k : 4 * k + 1024, :].astype(BF) for k in range(4)], axis=1)
+        qo[...] = _dot(stack, eo_ref[...]).astype(BF)
 
         def encode(c, carry):
             small = []
             for n in range(4):
                 r0 = pl.multiple_of(128 * c + 32 * n, 32)
                 patches = side_by_side(qo[pl.ds(r0, 16), :], qo[pl.ds(r0 + 16, 16), :], extra_ref[1, 1])
-                own4 = jnp.maximum(_dot(wq[0:256, :], patches).astype(BF), 0)
-                fown[s, :, pl.ds(pl.multiple_of(1024 * c + 256 * n, 256), 256)] = own4[0:64, :]
-                small += [own4[:, 0:32], own4[:, 128:160]]
-            pre = _dot(w2_ref[...], jnp.concatenate(small, axis=1))
+                got = jnp.maximum(_dot(wq[0:64, :], patches).astype(BF), 0)
+                fown[s, :, pl.ds(pl.multiple_of(1024 * c + 256 * n, 256), 256)] = got
+                small += [patches[:, 0:32], patches[:, 128:160]]
+            own4 = jnp.maximum(_dot(wq[0:256, :], jnp.concatenate(small, axis=1)).astype(BF), 0)
+            pre = _dot(w2_ref[...], own4)
             pre = jnp.maximum(pre + jnp.concatenate([bias2[...]] * 2, axis=1), 0.0)
             cown[s, :, pl.ds(pl.multiple_of(256 * c, 256), 256)] = pre.astype(BF)
             return carry
@@ -302,10 +301,11 @@
     loads[2].wait()
 
     def section(s, carry):
-        pad[0:96, 0:1024] = j_ref[s].astype(F32)
-        wide = pad[...]
-        stack = jnp.concatenate([pltpu.roll(wide, (17 - 2 * k) % 1152, 1) for k in range(4)], axis=0)
-        qp[...] = _dot(stack.T.astype(BF), ep_ref[...])[0:1056].astype(BF)
+        wide = jnp.concatenate([j_ref[s].astype(F32), jnp.zeros((96, 128), F32)], axis=1)
+        turned = jnp.concatenate([pltpu.roll(wide, 17, 1), jnp.zeros((32, 1152), F32)], axis=0)
+        tall[...] = turned.T
+        stack = jnp.concatenate([tall[2 * k : 2 * k + 1056, :].astype(BF) for k in range(4)], axis=1)
+        qp[...] = _dot(stack, ep_ref[...]).astype(BF)
 
         def partner(g, carry):
             r0 = pl.multiple_of(32 * g, 32)
@@ -391,7 +391,7 @@
             obuf[pl.ds(pl.multiple_of(144 * s, 16), 144), pl.ds(pl.multiple_of(128 * c, 128), 128)] = gram.astype(BF)
             return carry
 
-        lax.fori_loop(0, 16, block, 0, unroll=2)
+        lax.fori_loop(0, 16, block, 0, unroll=4)
 
         got = lax.dot_general(
             jnp.concatenate(_split3(mpx[...]), axis=0), perm_ref[...], (((1,), (1,)), ((), ())),
@@ -453,10 +453,10 @@
             pltpu.VMEM((8, 8, 256), F32),
             pltpu.VMEM((8, 8, 256), F32),
             pltpu.VMEM((8, 256), F32),
-            pltpu.VMEM((384, 768), BF),
+            pltpu.VMEM((512, 768), BF),
             pltpu.VMEM((512, 768), BF),
             pltpu.VMEM((1024, 1024), BF),
-            pltpu.VMEM((96, 1152), F32),
+            pltpu.VMEM((1152, 128), F32),
             pltpu.VMEM((1056, 768), BF),
             pltpu.VMEM((1024, 768), BF),
             pltpu.VMEM((256, PT * 128), BF),

time: 56.7 us -> 52 us (0.917)
  the two profiles are of different devices: /device:TPU:0 before, /device:TPU:15 now
where the time goes in v4:
time: 52 us; the launch traced here: 51.7 us
  Pallas kernels  51.1 us (98%)
  between operations  0.64 us (1%)
    pallas_call x1, Pallas kernels, local(): pl.pallas_call(_kernel, out_shape=(jax.ShapeDtypeStruct((2, 81, 8, 256),...  49.1 us
    pallas_call x1, Pallas kernels, local(): pl.pallas_call(_hand_on, out_shape=tuple((jax.ShapeDtypeStruct(r.shape, r...  2.02 us

profile of v4, /device:TPU:15, one launch (start us, length us, event | category | flops | bytes accessed | tf_op | source)
XLA Modules:
  0.0 51.7 jit_solution(8840395044816813631)
XLA Ops:
  0.6 49.1 %align.1 = (bf16[2,81,8,256]{3,2,1,0:T(8,128)(2,1)}, f32[2,16,512]{2,1,0:T(8,128)}, f32[2,2,32]{2,1,0:T(2,128)}) custom-call(s32[2]{0:T(128)} %pr_ref.1, s32[1,2]{1,0:T(1,128)} %bitcast.5, bf16[2,32,1024]{2,1,0:T(8,128)(2,1)} %img_ref.1, s32[2,2,16,512]{3,2,1,0:T(8,128)} %sh_ref.1, f32[2,2,16,512]{3,2,1,0:T(8,128)} %fr_ref.1, s32[2,2,256]{2,1,0:T(2,128)} %ends_ref.1, ...), custom_call_target="tpu_custom_call" | custom-call | tf_op jit(solution)/shard_map/align/pallas_call | solution.py:439
  49.7 2.0 %hand_on.1 = (bf16[2,81,8,256]{3,2,1,0:T(8,128)(2,1)}, f32[2,16,512]{2,1,0:T(8,128)}, f32[2,2,32]{2,1,0:T(2,128)}) custom-call(bf16[2,81,8,256]{3,2,1,0:T(8,128)(2,1)} %get-tuple-element.6.a, f32[2,16,512]{2,1,0:T(8,128)} %get-tuple-element.7.b, f32[2,2,32]{2,1,0:T(2,128)} %get-tuple-element.8.c), custom_call_target="tpu_custom_call" | custom-call | tf_op jit(solution)/shard_map/hand_on/pallas_call | solution.py:485

commit v5 on v4

--- a/solution.py
+++ b/solution.py
@@ -99,7 +99,7 @@
     pr_ref, cnt_ref, img_ref, sh_ref, fr_ref, ends_ref, stiff_ref, w1_ref, b1_ref, w2_ref, b2_ref,
     wsel_ref, wconst_ref, extra_ref, cmask_ref, home_ref, perm_ref, ep_hbm, eo_hbm, unflat_hbm,
     corr_ref, mis_ref, force_ref,
-    j_ref, i_ref, rbuf, anch, gbuf, pbuf, pstage, ep_ref, eo_ref, unflat_ref,
+    j_ref, i_ref, ask_out, ask_in, sbuf, rbuf, anch, gbuf, pbuf, pstage, ep_ref, eo_ref, unflat_ref,
     tall, qp, qo, p4, cpt, obuf, cbuf, wq, bias2, tbuf, px, mpx, fown, cown,
     send_sem, recv_sem, load_sem,
 ):
@@ -166,7 +166,6 @@
         px[s, 3] = (got[224:256] + got[192:224]) + got[160:192]
         return carry
 
-    lax.fori_loop(0, 2, pixels, 0)
 
     pl.semaphore_wait(barrier, 11)
 
@@ -176,10 +175,15 @@
             device_id=target, device_id_type=MESH,
         )
 
-    near = remote(img_ref, rbuf.at[0], 0, (back1, tile))
-    far = remote(img_ref, rbuf.at[1], 1, (back2, tile))
-    far.start()
-    near.start()
+    first_near = lax.shift_right_logical(pr_ref[0], 1) == fwd1
+    slots = [lax.bitwise_and(pr_ref[s], 1) for s in range(2)]
+    ask_out[0] = jnp.full((8, 128), jnp.where(first_near, slots[0], slots[1]), jnp.int32)
+    ask_out[1] = jnp.full((8, 128), jnp.where(first_near, slots[1], slots[0]), jnp.int32)
+    asks = [remote(ask_out.at[k], ask_in.at[k], 22 + k, (ahead, tile)) for k, ahead in enumerate((fwd1, fwd2))]
+    for c in asks:
+        c.start()
+    near = remote(sbuf.at[0], rbuf.at[0], 0, (back1, tile))
+    far = remote(sbuf.at[1], rbuf.at[1], 1, (back2, tile))
     down_tile = (sec, lax.rem(tile + 1, 8))
     up_tile = (sec, lax.rem(tile + 7, 8))
     own_down = remote(img_ref.at[:, 16:32], i_ref.at[:, 0:16], 2, down_tile)
@@ -201,6 +205,14 @@
     def _():
         i_ref[:, 48:64, :] = jnp.zeros((2, 16, 1024), BF)
         j_ref[:, 64:96, :] = jnp.zeros((2, 32, 1024), BF)
+
+    lax.fori_loop(0, 2, pixels, 0)
+
+    for k, copy in ((1, far), (0, near)):
+        asks[k].wait()
+        slot = jnp.broadcast_to(jnp.concatenate([ask_in[k, 0:1, :]] * 8, axis=1), (32, 1024))
+        sbuf[k] = jnp.where(slot == 0, img_ref[0].astype(F32), img_ref[1].astype(F32)).astype(BF)
+        copy.start()
 
     for c in anchor_sends:
         c.wait()
@@ -273,10 +285,8 @@
     near.wait()
     far.wait()
     for s in range(2):
-        p = pr_ref[s]
-        which = jnp.where(lax.shift_right_logical(p, 1) == fwd1, 0, 1)
-        slot = lax.bitwise_and(p, 1)
-        j_ref[s, 32:64, :] = rbuf[which, slot]
+        which = jnp.where(lax.shift_right_logical(pr_ref[s], 1) == fwd1, 0, 1)
+        j_ref[s, 32:64, :] = rbuf[which]
     part_down = remote(j_ref.at[:, 32:64], j_ref.at[:, 0:32], 12, down_tile)
     part_up = remote(j_ref.at[:, 32:64], j_ref.at[:, 64:96], 13, up_tile)
     pl.when(has_down)(part_down.start)
@@ -448,7 +458,10 @@
         scratch_shapes=[
             pltpu.VMEM((2, 96, 1024), BF),
             pltpu.VMEM((2, 64, 1024), BF),
-            pltpu.VMEM((2, 2, 32, 1024), BF),
+            pltpu.VMEM((2, 8, 128), jnp.int32),
+            pltpu.VMEM((2, 8, 128), jnp.int32),
+            pltpu.VMEM((2, 32, 1024), BF),
+            pltpu.VMEM((2, 32, 1024), BF),
             pltpu.VMEM((8, 256), F32),
             pltpu.VMEM((8, 8, 256), F32),
             pltpu.VMEM((8, 8, 256), F32),
@@ -470,8 +483,8 @@
             pltpu.VMEM((32, 256), F32),
             pltpu.VMEM((2, 64, 8192), BF),
             pltpu.VMEM((2, 64, 2048), BF),
-            pltpu.SemaphoreType.DMA((22,)),
-            pltpu.SemaphoreType.DMA((22,)),
+            pltpu.SemaphoreType.DMA((24,)),
+            pltpu.SemaphoreType.DMA((24,)),
             pltpu.SemaphoreType.DMA((3,)),
         ],
         compiler_params=pltpu.CompilerParams(

time: 52 us -> 53.4 us (1.027); the launches traced: 51.7 us -> 52.4 us
  Pallas kernels: 51.1 us -> 51.8 us
    pallas_call x1, Pallas kernels: 49.1 us -> 49.8 us  [local(): pl.pallas_call(_kernel, out_shape=(jax.ShapeDtypeStruct((2, 81, 8, 256),...]
where the time goes in v5:
time: 53.4 us; the launch traced here: 52.4 us
  Pallas kernels  51.8 us (97%)
  between operations  0.64 us (1%)
    pallas_call x1, Pallas kernels, local(): pl.pallas_call(_kernel, out_shape=(jax.ShapeDtypeStruct((2, 81, 8, 256),...  49.8 us
    pallas_call x1, Pallas kernels, local(): pl.pallas_call(_hand_on, out_shape=tuple((jax.ShapeDtypeStruct(r.shape, r...  2.02 us

profile of v5, /device:TPU:15, one launch (start us, length us, event | category | flops | bytes accessed | tf_op | source)
XLA Modules:
  0.0 52.4 jit_solution(16738649949382763621)
XLA Ops:
  0.6 49.8 %align.1 = (bf16[2,81,8,256]{3,2,1,0:T(8,128)(2,1)}, f32[2,16,512]{2,1,0:T(8,128)}, f32[2,2,32]{2,1,0:T(2,128)}) custom-call(s32[2]{0:T(128)} %pr_ref.1, s32[1,2]{1,0:T(1,128)} %bitcast.5, bf16[2,32,1024]{2,1,0:T(8,128)(2,1)} %img_ref.1, s32[2,2,16,512]{3,2,1,0:T(8,128)} %sh_ref.1, f32[2,2,16,512]{3,2,1,0:T(8,128)} %fr_ref.1, s32[2,2,256]{2,1,0:T(2,128)} %ends_ref.1, ...), custom_call_target="tpu_custom_call" | custom-call | tf_op jit(solution)/shard_map/align/pallas_call | solution.py:449
  50.4 2.0 %hand_on.1 = (bf16[2,81,8,256]{3,2,1,0:T(8,128)(2,1)}, f32[2,16,512]{2,1,0:T(8,128)}, f32[2,2,32]{2,1,0:T(2,128)}) custom-call(bf16[2,81,8,256]{3,2,1,0:T(8,128)(2,1)} %get-tuple-element.6.a, f32[2,16,512]{2,1,0:T(8,128)} %get-tuple-element.7.b, f32[2,2,32]{2,1,0:T(2,128)} %get-tuple-element.8.c), custom_call_target="tpu_custom_call" | custom-call | tf_op jit(solution)/shard_map/hand_on/pallas_call | solution.py:498

commit v6 on v4

--- a/solution.py
+++ b/solution.py
@@ -37,6 +37,12 @@
                     for v in range(4):
                         wsel[e, ta, tb, 4 * u + v, (u + 2 * ta) * 16 + 8 * e + 2 * tb + v] = 1
                 wconst[e, ta, tb, 0, 96 + 4 * e + 2 * ta + tb] = BIG
+    wown = np.zeros((2, 2, 16, 64), np.float32)
+    for ta in range(2):
+        for tb in range(2):
+            for u in range(4):
+                for v in range(4):
+                    wown[ta, tb, 4 * u + v, (u + 2 * ta) * 8 + 2 * tb + v] = 1
     extra = np.zeros((3, 3, 16, 256), np.float32)
     cmask = np.zeros((3, 3, 8, 128), np.float32)
     for tk in range(3):
@@ -76,6 +82,7 @@
         wsel=wsel.reshape(8, 16, 112),
         wconst=wconst.reshape(8, 1, 112),
         extra=extra,
+        wown=wown.reshape(4, 16, 64),
         cmask=cmask,
         unflat=unflat,
         home=home,
@@ -97,10 +104,10 @@
 
 def _kernel(
     pr_ref, cnt_ref, img_ref, sh_ref, fr_ref, ends_ref, stiff_ref, w1_ref, b1_ref, w2_ref, b2_ref,
-    wsel_ref, wconst_ref, extra_ref, cmask_ref, home_ref, perm_ref, ep_hbm, eo_hbm, unflat_hbm,
+    wsel_ref, wown_ref, wconst_ref, extra_ref, cmask_ref, home_ref, perm_ref, ep_hbm, eo_hbm, unflat_hbm,
     corr_ref, mis_ref, force_ref,
     j_ref, i_ref, rbuf, anch, gbuf, pbuf, pstage, ep_ref, eo_ref, unflat_ref,
-    tall, qp, qo, p4, cpt, obuf, cbuf, wq, bias2, tbuf, px, mpx, fown, cown,
+    tall, qp, qo, p4, cpt, obuf, cbuf, wq, wo, bias2, tbuf, px, mpx, fown, cown,
     send_sem, recv_sem, load_sem,
 ):
     sec = lax.axis_index("sec")
@@ -146,6 +153,11 @@
             w1_ref[...], wsel_ref[m], (((0,), (0,)), ((), ())), preferred_element_type=F32
         )
         wq[64 * m : 64 * m + 64, :] = (spread + base + wconst_ref[m]).astype(BF)
+    for m in range(4):
+        spread = lax.dot_general(
+            w1_ref[...], wown_ref[m], (((0,), (0,)), ((), ())), preferred_element_type=F32
+        )
+        wo[64 * m : 64 * m + 64, :] = (spread + base[:, 48:112]).astype(BF)
     bias2[...] = jnp.broadcast_to(b2_ref[...], (128, 64)).T
 
     lane128 = lax.broadcasted_iota(jnp.int32, (1, 128), 1)
@@ -249,24 +261,27 @@
         wide = jnp.concatenate([i_ref[s].astype(F32), jnp.zeros((64, 128), F32)], axis=1)
         turned = jnp.concatenate([pltpu.roll(wide, 1, 1), pltpu.roll(wide, 1151, 1)], axis=0)
         tall[...] = turned.T
-        stack = jnp.concatenate([tall[4 * k : 4 * k + 1024, :].astype(BF) for k in range(4)], axis=1)
-        qo[...] = _dot(stack, eo_ref[...]).astype(BF)
+        stack = [tall[4 * k : 4 * k + 1024, :].reshape(64, 16, 128)[:, 0:8, :].reshape(512, 128) for k in range(4)]
+        stack = jnp.concatenate([x.astype(BF) for x in stack], axis=1)
+        qo[...] = _dot(stack, eo_ref[...])
+
+        ones = extra_ref[1, 1].astype(F32)
 
         def encode(c, carry):
             small = []
             for n in range(4):
-                r0 = pl.multiple_of(128 * c + 32 * n, 32)
-                patches = side_by_side(qo[pl.ds(r0, 16), :], qo[pl.ds(r0 + 16, 16), :], extra_ref[1, 1])
-                got = jnp.maximum(_dot(wq[0:64, :], patches).astype(BF), 0)
+                r0 = pl.multiple_of(64 * c + 16 * n, 16)
+                patches = side_by_side(qo[pl.ds(r0, 8), :], qo[pl.ds(r0 + 8, 8), :], ones).astype(BF)
+                got = jnp.maximum(_dot(wo[0:64, :], patches).astype(BF), 0)
                 fown[s, :, pl.ds(pl.multiple_of(1024 * c + 256 * n, 256), 256)] = got
                 small += [patches[:, 0:32], patches[:, 128:160]]
-            own4 = jnp.maximum(_dot(wq[0:256, :], jnp.concatenate(small, axis=1)).astype(BF), 0)
+            own4 = jnp.maximum(_dot(wo[...], jnp.concatenate(small, axis=1)).astype(BF), 0)
             pre = _dot(w2_ref[...], own4)
             pre = jnp.maximum(pre + jnp.concatenate([bias2[...]] * 2, axis=1), 0.0)
             cown[s, :, pl.ds(pl.multiple_of(256 * c, 256), 256)] = pre.astype(BF)
             return carry
 
-        return lax.fori_loop(0, 8, encode, carry, unroll=4)
+        return lax.fori_loop(0, 8, encode, carry, unroll=8)
 
     own(0, 0)
 
@@ -336,7 +351,7 @@
 
         for n in range(4):
             partner(n, 0)
-        lax.fori_loop(1, QUADS // 4, both, 0)
+        lax.fori_loop(1, QUADS // 4, both, 0, unroll=7)
         coarsen(QUADS - 5, 4)
         partner(QUADS - 1, 0)
         coarsen(QUADS - 1, 1)
@@ -432,7 +447,7 @@
     sm = pl.BlockSpec(memory_space=pltpu.SMEM)
     hbm = pl.BlockSpec(memory_space=pl.ANY)
     consts = [
-        jnp.asarray(t["wsel"], BF), jnp.asarray(t["wconst"], F32), jnp.asarray(t["extra"], BF),
+        jnp.asarray(t["wsel"], BF), jnp.asarray(t["wown"], BF), jnp.asarray(t["wconst"], F32), jnp.asarray(t["extra"], BF),
         jnp.asarray(t["cmask"], F32), jnp.asarray(t["home"], F32), jnp.asarray(t["perm"], BF),
         jnp.asarray(t["ep"], BF), jnp.asarray(t["eo"], BF), jnp.asarray(t["unflat"], BF),
     ]
@@ -443,7 +458,7 @@
             jax.ShapeDtypeStruct((2, 16, 512), F32),
             jax.ShapeDtypeStruct((2, 2, 32), F32),
         ),
-        in_specs=[sm, sm] + [vm] * 15 + [hbm] * 3,
+        in_specs=[sm, sm] + [vm] * 16 + [hbm] * 3,
         out_specs=(vm, vm, vm),
         scratch_shapes=[
             pltpu.VMEM((2, 96, 1024), BF),
@@ -458,12 +473,13 @@
             pltpu.VMEM((1024, 1024), BF),
             pltpu.VMEM((1152, 128), F32),
             pltpu.VMEM((1056, 768), BF),
-            pltpu.VMEM((1024, 768), BF),
+            pltpu.VMEM((512, 768), F32),
             pltpu.VMEM((256, PT * 128), BF),
             pltpu.VMEM((PT * 32, 128), BF),
             pltpu.VMEM((288, 2048), BF),
             pltpu.VMEM((2, 648, 128), F32),
             pltpu.VMEM((512, 112), BF),
+            pltpu.VMEM((256, 64), BF),
             pltpu.VMEM((64, 128), F32),
             pltpu.VMEM((512, 128), F32),
             pltpu.VMEM((2, 4, 32, 256), F32),

time: 52 us -> 48.3 us (0.929)
  Pallas kernels: 51.1 us -> 47.3 us
    pallas_call x1, Pallas kernels: 49.1 us -> 45.3 us  [local(): pl.pallas_call(_kernel, out_shape=(jax.ShapeDtypeStruct((2, 81, 8, 256),...]
where the time goes in v6:
time: 48.3 us; the launch traced here: 48 us
  Pallas kernels  47.3 us (98%)
  between operations  0.64 us (1%)
    pallas_call x1, Pallas kernels, local(): pl.pallas_call(_kernel, out_shape=(jax.ShapeDtypeStruct((2, 81, 8, 256),...  45.3 us
    pallas_call x1, Pallas kernels, local(): pl.pallas_call(_hand_on, out_shape=tuple((jax.ShapeDtypeStruct(r.shape, r...  2.02 us

profile of v6, /device:TPU:15, one launch (start us, length us, event | category | flops | bytes accessed | tf_op | source)
XLA Modules:
  0.0 48.0 jit_solution(18109487506405109879)
XLA Ops:
  0.6 45.3 %align.1 = (bf16[2,81,8,256]{3,2,1,0:T(8,128)(2,1)}, f32[2,16,512]{2,1,0:T(8,128)}, f32[2,2,32]{2,1,0:T(2,128)}) custom-call(s32[2]{0:T(128)} %pr_ref.1, s32[1,2]{1,0:T(1,128)} %bitcast.5, bf16[2,32,1024]{2,1,0:T(8,128)(2,1)} %img_ref.1, s32[2,2,16,512]{3,2,1,0:T(8,128)} %sh_ref.1, f32[2,2,16,512]{3,2,1,0:T(8,128)} %fr_ref.1, s32[2,2,256]{2,1,0:T(2,128)} %ends_ref.1, ...), custom_call_target="tpu_custom_call" | custom-call | tf_op jit(solution)/shard_map/align/pallas_call | solution.py:454
  45.9 2.0 %hand_on.1 = (bf16[2,81,8,256]{3,2,1,0:T(8,128)(2,1)}, f32[2,16,512]{2,1,0:T(8,128)}, f32[2,2,32]{2,1,0:T(2,128)}) custom-call(bf16[2,81,8,256]{3,2,1,0:T(8,128)(2,1)} %get-tuple-element.6.a, f32[2,16,512]{2,1,0:T(8,128)} %get-tuple-element.7.b, f32[2,2,32]{2,1,0:T(2,128)} %get-tuple-element.8.c), custom_call_target="tpu_custom_call" | custom-call | tf_op jit(solution)/shard_map/hand_on/pallas_call | solution.py:501

commit v7 on v6

--- a/solution.py
+++ b/solution.py
@@ -406,7 +406,7 @@
             obuf[pl.ds(pl.multiple_of(144 * s, 16), 144), pl.ds(pl.multiple_of(128 * c, 128), 128)] = gram.astype(BF)
             return carry
 
-        lax.fori_loop(0, 16, block, 0, unroll=4)
+        lax.fori_loop(0, 16, block, 0, unroll=16)
 
         got = lax.dot_general(
             jnp.concatenate(_split3(mpx[...]), axis=0), perm_ref[...], (((1,), (1,)), ((), ())),

time: 48.3 us -> 46.3 us (0.959)
  Pallas kernels: 47.3 us -> 45.3 us
    pallas_call x1, Pallas kernels: 45.3 us -> 43.3 us  [local(): pl.pallas_call(_kernel, out_shape=(jax.ShapeDtypeStruct((2, 81, 8, 256),...]
where the time goes in v7:
time: 46.3 us; the launch traced here: 46 us
  Pallas kernels  45.3 us (98%)
  between operations  0.64 us (1%)
    pallas_call x1, Pallas kernels, local(): pl.pallas_call(_kernel, out_shape=(jax.ShapeDtypeStruct((2, 81, 8, 256),...  43.3 us
    pallas_call x1, Pallas kernels, local(): pl.pallas_call(_hand_on, out_shape=tuple((jax.ShapeDtypeStruct(r.shape, r...  2.02 us

profile of v7, /device:TPU:15, one launch (start us, length us, event | category | flops | bytes accessed | tf_op | source)
XLA Modules:
  0.0 46.0 jit_solution(4279801241138869246)
XLA Ops:
  0.6 43.3 %align.1 = (bf16[2,81,8,256]{3,2,1,0:T(8,128)(2,1)}, f32[2,16,512]{2,1,0:T(8,128)}, f32[2,2,32]{2,1,0:T(2,128)}) custom-call(s32[2]{0:T(128)} %pr_ref.1, s32[1,2]{1,0:T(1,128)} %bitcast.5, bf16[2,32,1024]{2,1,0:T(8,128)(2,1)} %img_ref.1, s32[2,2,16,512]{3,2,1,0:T(8,128)} %sh_ref.1, f32[2,2,16,512]{3,2,1,0:T(8,128)} %fr_ref.1, s32[2,2,256]{2,1,0:T(2,128)} %ends_ref.1, ...), custom_call_target="tpu_custom_call" | custom-call | tf_op jit(solution)/shard_map/align/pallas_call | solution.py:454
  43.9 2.0 %hand_on.1 = (bf16[2,81,8,256]{3,2,1,0:T(8,128)(2,1)}, f32[2,16,512]{2,1,0:T(8,128)}, f32[2,2,32]{2,1,0:T(2,128)}) custom-call(bf16[2,81,8,256]{3,2,1,0:T(8,128)(2,1)} %get-tuple-element.6.a, f32[2,16,512]{2,1,0:T(8,128)} %get-tuple-element.7.b, f32[2,2,32]{2,1,0:T(2,128)} %get-tuple-element.8.c), custom_call_target="tpu_custom_call" | custom-call | tf_op jit(solution)/shard_map/hand_on/pallas_call | solution.py:501

commit v8 on v7

--- a/solution.py
+++ b/solution.py
@@ -178,7 +178,7 @@
         px[s, 3] = (got[224:256] + got[192:224]) + got[160:192]
         return carry
 
-    lax.fori_loop(0, 2, pixels, 0)
+    lax.fori_loop(0, 2, pixels, 0, unroll=2)
 
     pl.semaphore_wait(barrier, 11)
 
@@ -419,7 +419,7 @@
 
         return carry
 
-    lax.fori_loop(0, 2, section, 0)
+    lax.fori_loop(0, 2, section, 0, unroll=2)
 
     for h in range(2):
         flat = _dot(obuf[:, 1024 * h : 1024 * h + 1024], unflat_ref[...])

time: 46.3 us -> 45.9 us (level)
  Pallas kernels: 45.3 us -> 44.7 us
    pallas_call x1, Pallas kernels: 43.3 us -> 42.7 us  [local(): pl.pallas_call(_kernel, out_shape=(jax.ShapeDtypeStruct((2, 81, 8, 256),...]
where the time goes in v8:
time: 45.9 us; the launch traced here: 45.3 us
  Pallas kernels  44.7 us (97%)
  between operations  0.64 us (1%)
    pallas_call x1, Pallas kernels, local(): pl.pallas_call(_kernel, out_shape=(jax.ShapeDtypeStruct((2, 81, 8, 256),...  42.7 us
    pallas_call x1, Pallas kernels, local(): pl.pallas_call(_hand_on, out_shape=tuple((jax.ShapeDtypeStruct(r.shape, r...  2.02 us

profile of v8, /device:TPU:15, one launch (start us, length us, event | category | flops | bytes accessed | tf_op | source)
XLA Modules:
  0.0 45.3 jit_solution(4304805869385835086)
XLA Ops:
  0.6 42.7 %align.1 = (bf16[2,81,8,256]{3,2,1,0:T(8,128)(2,1)}, f32[2,16,512]{2,1,0:T(8,128)}, f32[2,2,32]{2,1,0:T(2,128)}) custom-call(s32[2]{0:T(128)} %pr_ref.1, s32[1,2]{1,0:T(1,128)} %bitcast.5, bf16[2,32,1024]{2,1,0:T(8,128)(2,1)} %img_ref.1, s32[2,2,16,512]{3,2,1,0:T(8,128)} %sh_ref.1, f32[2,2,16,512]{3,2,1,0:T(8,128)} %fr_ref.1, s32[2,2,256]{2,1,0:T(2,128)} %ends_ref.1, ...), custom_call_target="tpu_custom_call" | custom-call | tf_op jit(solution)/shard_map/align/pallas_call | solution.py:454
  43.3 2.0 %hand_on.1 = (bf16[2,81,8,256]{3,2,1,0:T(8,128)(2,1)}, f32[2,16,512]{2,1,0:T(8,128)}, f32[2,2,32]{2,1,0:T(2,128)}) custom-call(bf16[2,81,8,256]{3,2,1,0:T(8,128)(2,1)} %get-tuple-element.6.a, f32[2,16,512]{2,1,0:T(8,128)} %get-tuple-element.7.b, f32[2,2,32]{2,1,0:T(2,128)} %get-tuple-element.8.c), custom_call_target="tpu_custom_call" | custom-call | tf_op jit(solution)/shard_map/hand_on/pallas_call | solution.py:501
